TPU v7x, 256 devices: a whole 4x4x8 slice. The times are simulated.
256 devices in a mesh: ga: 16 (over z, x_lo), ba: 16 (over y, x_hi, core).
Axes of the slice: x: 4 (x_hi: 2, x_lo: 2; x = x_hi * 2 + x_lo), y: 4, z: 8, core: 2. Of those that a mesh axis runs over, the one named last changes fastest.
Arguments:
- matrix_elements: bfloat16 [256, 64, 8192], P('ba', None, 'ga'), may hold values from -0.0625 to 0.0625
- screening: bfloat16 [8192, 8192], P(None, 'ga'), may hold values from -1 to 2
- band_factor: float32 [2, 256], P(None, 'ba'), may hold values from 0.5 to 5
- pair_list: int32 [2, 2016], replicated, may hold values from 0 to 63, as said below
Outputs:
- sigma: float32 [2, 2016], P(None, 'ga')
Inputs may be any that keep to these rules, and one draw needn't show every extreme that they name: `pair_list`: each column is a pair (m, n) with m < n; every such pair of the 64 bands appears exactly once.
All inputs are finite; a program needn't handle non-finite values.
Results may differ from a plain program's by a relative error of at most 0.0003.
Values may be sent and summed in bfloat16 or wider, within the bound.
A program may use at most 128 MiB of HBM per device.

v0:
```python
import jax
import jax.numpy as jnp
from jax import lax
from jax.sharding import PartitionSpec as P


def shards(matrix_elements, screening, band_factor, pair_list):
    band_count, quasi_count, block_width = matrix_elements.shape
    flattened = matrix_elements.reshape(band_count * quasi_count, block_width)
    elements_wide = matrix_elements.astype(jnp.float32)
    all_elements = lax.all_gather(flattened, "ga", axis=1, tiled=True)
    applied = jnp.dot(all_elements, screening, preferred_element_type=jnp.float32)
    per_band = jnp.einsum(
        "vmg,vng->vmn",
        applied.reshape(band_count, quasi_count, block_width),
        elements_wide,
        precision=lax.Precision.HIGHEST,
    )
    local_sigma = jnp.einsum("fv,vmn->fmn", band_factor, per_band, precision=lax.Precision.HIGHEST)
    freq_count = local_sigma.shape[0]
    matrix_flat = local_sigma.reshape(freq_count, quasi_count * quasi_count)
    flat_index = pair_list[0] * quasi_count + pair_list[1]
    summed = lax.psum(matrix_flat, ("ga", "ba"))
    owned = pair_list.shape[1] // lax.axis_size("ga")
    own_pairs = lax.dynamic_slice_in_dim(flat_index, lax.axis_index("ga") * owned, owned, 0)
    return jnp.take(summed, own_pairs, axis=1)


def solution(mesh):
    placed = (P("ba", None, "ga"), P(None, "ga"), P(None, "ba"), P())
    return jax.shard_map(
        shards, mesh=mesh, in_specs=placed, out_specs=P(None, "ga"), check_vma=False
    )
```

profile of v0, /device:TPU:1, one launch (start us, length us, event | category | flops | bytes accessed | tf_op | source)
XLA Modules:
  0.0 483.4 jit_solution(13697610732787808559)
XLA Ops:
  6.5 0.0 copy-start
  6.5 0.0 all-gather.2.cloned.1.call-start
  6.5 0.7 all-gather.2.cloned.1.call-update
  7.3 0.8 fusion.3
  8.1 0.1 compare_and_fusion
  8.2 0.0 copy-start.1
  8.2 355.8 %all-gather.2.cloned.1.call-done = bf16[1024,8192]{1,0:T(8,128)(2,1)} async-done(((bf16[1024,512]{1,0:T(8,128)(2,1)}), bf16[1024,8192]{1,0:T(8,128)(2,1)}) %all-gather.2.cloned.1.call-update) | async-done | bytes 16777232 | tf_op jit(solution)/shard_map/all_gather | solution.py:11
  364.0 14.3 %fusion.4 = f32[1024,512]{1,0:T(8,128)S(1)} fusion(bf16[1024,8192]{1,0:T(8,128)(2,1)} %all-gather.2.cloned.1.call-done, bf16[8192,512]{1,0:T(8,128)(2,1)} %param.5), kind=kOutput, calls=%fused_computation.12 | convolution fusion | flops 8589934592 | bytes 27262976 | tf_op jit(solution)/shard_map/dot_general | solution.py:12
  378.3 0.0 copy-done.1
  378.3 1.2 fusion.5
  379.5 0.0 copy-done
  379.5 0.7 convolution_bitcast_fusion
  380.2 0.7 copy.10
  380.9 92.7 %psum.7 = f32[2,4096]{0,1:T(8,128)} all-reduce(f32[2,4096]{0,1:T(8,128)S(1)} %bitcast.19), channel_id=1, replica_groups=mesh['ga'=16,'ba'=16] {'ga','ba'}, use_global_device_ids=true, to_apply=%region_0.0 | all-reduce | flops 8192 | bytes 65536 | tf_op jit(solution)/shard_map/psum | solution.py:23
  473.6 2.2 gather_fusion
  475.8 0.1 select_bitcast_fusion
  475.9 0.6 copy.8
  (1 shorter events, 0.0 us)
Async XLA Ops:
  6.5 372.9 %copy-start = (f32[2,16]{1,0:T(2,128)S(1)}, f32[2,16]{1,0:T(2,128)}, u32[]{:S(2)}) copy-start(f32[2,16]{1,0:T(2,128)} %param.6) | copy-start | bytes 388
  6.5 357.4 %all-gather.2.cloned.1.call-start = ((), (), s32[]{:S(2)}) async-start(), calls=%async_computation | async-start | bytes 17825792 | tf_op jit(solution)/shard_map/all_gather | solution.py:11
  8.2 370.1 %copy-start.1 = (bf16[16,64,512]{2,1,0:T(8,128)(2,1)S(1)}, bf16[16,64,512]{2,1,0:T(8,128)(2,1)}, u32[]{:S(2)}) copy-start(bf16[16,64,512]{2,1,0:T(8,128)(2,1)} %param.4) | copy-start | bytes 3145732
Sparse Core Ops, SparseCore 0:
  9.2 354.7 all-gather.1
where the time goes:
time: 484 us; the launch traced here: 483 us
  waiting for transfers between devices  356 us (74%)
  blocking collectives  92.7 us (19%)
  matrix products  16.2 us (3%)
  between operations  13.5 us (3%)
    all_gather x1, waiting for transfers between devices, shards(): all_elements = lax.all_gather(flattened, 'ga', axis=1, tiled=True)  356 us
    psum x1, blocking collectives, shards(): summed = lax.psum(matrix_flat, ('ga', 'ba'))  92.7 us
    dot_general x1, matrix products, shards(): jnp.dot(all_elements, screening, preferred_element_type=jnp.float32)  14.3 us
  transfers between devices with their start and end apart: 1, of which 1 were waited for; matrix products, arithmetic and copies ran while one was open for 0% of the time, Pallas kernels for 0%

commit v1 on v0

v1 whole, which is shorter than its diff:
```python
import functools

import jax
import jax.numpy as jnp
from jax import lax
from jax.experimental import pallas as pl
from jax.experimental.pallas import tpu as pltpu
from jax.sharding import PartitionSpec as P

MESH = pl.DeviceIdType.MESH
GB = 512
CH = 256
NCH = 4
NBLK = 10
A0, A1, AM1, A2, AM2, B2 = range(6)
UP1, UP2, DN1, DN2, XF = range(5)
FOREIGN = (
    (A1, ((AM2, 0), (B2, 1))),
    (AM1, ((A2, 2), (B2, 3))),
    (AM2, ((A2, 4), (B2, 5))),
    (B2, ((A2, 6), (A1, 7), (A0, 8), (AM1, 9))),
)


def remote(src, dst, send, recv, device):
    return pltpu.make_async_remote_copy(
        src_ref=src, dst_ref=dst, send_sem=send, recv_sem=recv, device_id=device, device_id_type=MESH
    )


def wait_bytes(ref, sem):
    pltpu.make_async_copy(ref, ref, sem).wait()


def kernel(
    m_ref, w_ref, bf_ref, pair_ref, out_ref,
    mv, wown, wf, pp, one_n, facc, red_src, red_a, red_b,
    msend, mrecv, mloc, wloc, w1s, w1r, w2s, w2r, w3s, w3r, r1s, r1r, r2s, r2r,
):
    ga, ba = lax.axis_index("ga"), lax.axis_index("ba")
    z, s = ga // 2, lax.rem(ga, 2)
    y, xh, c = ba // 4, lax.rem(ba // 2, 2), lax.rem(ba, 2)

    def gai(dz, flip=0):
        side = 1 - s if flip else s
        return lax.rem(z + 8 + dz, 8) * 2 + side

    def bai(dy, dx, core):
        return (lax.rem(y + 4 + dy, 4) * 2 + lax.rem(xh + dx, 2)) * 2 + core

    barrier = pltpu.get_barrier_semaphore()

    @pl.loop(1, 16)
    def _(k):
        pl.semaphore_signal(barrier, inc=1, device_id=(lax.rem(ga + k, 16), ba), device_id_type=MESH)
        pl.semaphore_signal(barrier, inc=1, device_id=(ga, lax.rem(ba + k, 16)), device_id_type=MESH)

    own_m = pltpu.make_async_copy(m_ref, mv.at[A0], mloc)
    own_m.start()
    own_rows = ((A0, gai(0)), (A1, gai(1)), (AM1, gai(-1)), (A2, gai(2)), (AM2, gai(-2)), (B2, gai(2, 1)))
    own_w = []
    for slot, block in own_rows:
        cp = pltpu.make_async_copy(w_ref.at[pl.ds(block * GB, GB)], wown.at[slot], wloc.at[slot])
        cp.start()
        own_w.append(cp)

    pl.semaphore_wait(barrier, 30)

    w1 = []
    plan = (
        (gai(-1), ((gai(-3), 0), (gai(1, 1), 1))),
        (gai(1), ((gai(3), 2), (gai(3, 1), 3))),
        (gai(2), ((gai(4), 4), (gai(4, 1), 5))),
        (gai(-2, 1), ((gai(0, 1), 6), (gai(-1, 1), 7), (gai(-2, 1), 8), (gai(-3, 1), 9))),
    )
    for target, blocks in plan:
        for block, index in blocks:
            cp = remote(
                w_ref.at[pl.ds(block * GB + ba * 32, 32)], wf.at[ba, index], w1s, w1r, (target, ba)
            )
            cp.start()

    def hop(flow, k):
        rows = pl.ds(pl.multiple_of(k * CH, CH), CH)
        src, dst, target = {
            UP1: (m_ref, AM1, gai(1)),
            DN1: (m_ref, A1, gai(-1)),
            UP2: (mv.at[AM1], AM2, gai(1)),
            DN2: (mv.at[A1], A2, gai(-1)),
            XF: (mv.at[A2], B2, gai(0, 1)),
        }[flow]
        return remote(
            src.at[rows], mv.at[dst, rows], msend.at[flow, k], mrecv.at[flow, k], (target, ba)
        )

    @pl.loop(0, NCH)
    def _(k):
        hop(UP1, k).start()
        hop(DN1, k).start()

    pp[...] = jnp.full(pp.shape, -1, jnp.int32)
    for a in range(16):
        pp[:, a * 128 : a * 128 + 126] = pair_ref[:, a * 126 : (a + 1) * 126]
    band = lax.rem(lax.broadcasted_iota(jnp.int32, (256, 2048), 0), 64)
    one_n[...] = jnp.where(band == pp[1:2, :], 1.0, 0.0).astype(jnp.bfloat16)
    facc[...] = jnp.zeros_like(facc)

    wait_bytes(wf.at[ba], w1r)
    peers = [(q // 2, q % 2) for q in range(1, 8)]
    w2 = []
    for q, (dy, dx) in enumerate(peers):
        cp = remote(wf.at[ba], wf.at[ba], w2s.at[q], w2r.at[q], (ga, bai(dy, dx, c)))
        cp.start()
        w2.append(cp)
    cross = [remote(wf.at[ba], wf.at[ba], w3s.at[7], w3r.at[7], (ga, bai(0, 0, 1 - c)))]
    cross[0].start()

    @pl.loop(0, NCH)
    def _(k):
        hop(UP1, k).wait_recv()
        hop(UP2, k).start()
        hop(DN1, k).wait_recv()
        hop(DN2, k).start()

    for q, (dy, dx) in enumerate(peers):
        origin = bai(-dy, dx, c)
        w2[q].wait_recv()
        cp = remote(wf.at[origin], wf.at[origin], w3s.at[q], w3r.at[q], (ga, bai(0, 0, 1 - c)))
        cp.start()
        cross.append(cp)
    own_m.wait()
    for cp in own_w:
        cp.wait()
    for cp in cross:
        cp.wait_recv()

    lane = lax.broadcasted_iota(jnp.int32, (64, 256), 1) // 64

    def compute(k):
        rows = pl.ds(pl.multiple_of(k * CH, CH), CH)

        def second(col, applied):
            high = applied.astype(jnp.bfloat16)
            low = (applied - high.astype(jnp.float32)).astype(jnp.bfloat16)
            right = mv[col, rows, :]
            dims = (((1,), (1,)), ((), ()))
            return lax.dot_general(
                high, right, dims, preferred_element_type=jnp.float32
            ) + lax.dot_general(low, right, dims, preferred_element_type=jnp.float32)

        applied = jnp.zeros((CH, GB), jnp.float32)
        for slot in (A0, A1, AM1, A2, AM2, B2):
            applied += jnp.dot(mv[slot, rows, :], wown[slot], preferred_element_type=jnp.float32)
        per_band = second(A0, applied)
        for col, terms in FOREIGN:
            applied = jnp.zeros((CH, GB), jnp.float32)
            for slot, index in terms:
                block = wf[:, index].reshape(GB, GB)
                applied += jnp.dot(mv[slot, rows, :], block, preferred_element_type=jnp.float32)
            per_band += second(col, applied)
        for f in range(2):
            total = facc[pl.ds(f * 64, 64), :]
            for q in range(4):
                part = per_band[q * 64 : (q + 1) * 64, :]
                total += jnp.where(lane == q, part * bf_ref[f, k * 4 + q], 0.0)
            facc[pl.ds(f * 64, 64), :] = total

    @pl.loop(0, NCH + 1)
    def _(k):
        @pl.when(k < NCH)
        def _():
            hop(DN2, k).wait_recv()
            hop(XF, k).start()

        @pl.when(k >= 1)
        def _():
            hop(UP2, k - 1).wait_recv()
            hop(XF, k - 1).wait_recv()
            compute(k - 1)

    full = facc[...]
    x1 = full.astype(jnp.bfloat16)
    rest = full - x1.astype(jnp.float32)
    x2 = rest.astype(jnp.bfloat16)
    x3 = (rest - x2.astype(jnp.float32)).astype(jnp.bfloat16)
    picked = (
        jnp.dot(x1, one_n[...], preferred_element_type=jnp.float32)
        + jnp.dot(x2, one_n[...], preferred_element_type=jnp.float32)
        + jnp.dot(x3, one_n[...], preferred_element_type=jnp.float32)
    )
    first = lax.broadcasted_iota(jnp.int32, (64, 2048), 0) == pp[0:1, :]
    for f in range(2):
        row = jnp.sum(jnp.where(first, picked[f * 64 : (f + 1) * 64], 0.0), axis=0, keepdims=True)
        for a in range(16):
            red_src[a, f : f + 1, :] = row[:, a * 128 : (a + 1) * 128]

    @pl.loop(1, 16)
    def _(k):
        peer = lax.rem(ga + k, 16)
        remote(red_src.at[peer], red_a.at[k - 1], r1s, r1r, (peer, ba)).start()

    wait_bytes(red_a, r1r)
    mine = red_src[ga]
    for k in range(15):
        mine += red_a[k]
    red_b[ba] = mine

    @pl.loop(1, 16)
    def _(k):
        peer = lax.rem(ba + k, 16)
        remote(red_b.at[ba], red_b.at[ba], r2s, r2r, (ga, peer)).start()

    wait_bytes(red_b.at[pl.ds(0, 15)], r2r)
    total = red_b[0]
    for k in range(1, 16):
        total += red_b[k]
    out_ref[...] = total[:, :126]

    wait_bytes(wf.at[0], w1s)
    for cp in w2 + cross:
        cp.wait_send()

    @pl.loop(0, NCH)
    def _(k):
        for flow in (UP1, DN1, UP2, DN2, XF):
            hop(flow, k).wait_send()

    wait_bytes(red_a, r1s)
    wait_bytes(red_b.at[pl.ds(0, 15)], r2s)


def shards(matrix_elements, screening, band_factor, pair_list):
    bands, quasi, width = matrix_elements.shape
    dma = pltpu.SemaphoreType.DMA
    return pl.pallas_call(
        kernel,
        out_shape=jax.ShapeDtypeStruct((2, 126), jnp.float32),
        in_specs=[
            pl.BlockSpec(memory_space=pl.ANY),
            pl.BlockSpec(memory_space=pl.ANY),
            pl.BlockSpec(memory_space=pltpu.SMEM),
            pl.BlockSpec(memory_space=pltpu.VMEM),
        ],
        out_specs=pl.BlockSpec(memory_space=pltpu.VMEM),
        scratch_shapes=[
            pltpu.VMEM((6, 1024, GB), jnp.bfloat16),
            pltpu.VMEM((6, GB, GB), jnp.bfloat16),
            pltpu.VMEM((16, NBLK, 32, GB), jnp.bfloat16),
            pltpu.VMEM((2, 2048), jnp.int32),
            pltpu.VMEM((256, 2048), jnp.bfloat16),
            pltpu.VMEM((128, 256), jnp.float32),
            pltpu.VMEM((16, 2, 128), jnp.float32),
            pltpu.VMEM((15, 2, 128), jnp.float32),
            pltpu.VMEM((16, 2, 128), jnp.float32),
            dma((5, NCH)), dma((5, NCH)), dma, dma((6,)),
            dma, dma, dma((7,)), dma((7,)), dma((8,)), dma((8,)),
            dma, dma, dma, dma,
        ],
        compiler_params=pltpu.CompilerParams(
            collective_id=0, has_side_effects=True, vmem_limit_bytes=48 << 20
        ),
        cost_estimate=pl.CostEstimate(flops=9 * 10**9, bytes_accessed=20 << 20, transcendentals=0),
        name="self_energy",
    )(matrix_elements.reshape(bands * quasi, width), screening, band_factor, pair_list)


def solution(mesh):
    placed = (P("ba", None, "ga"), P(None, "ga"), P(None, "ba"), P())
    return jax.shard_map(
        shards, mesh=mesh, in_specs=placed, out_specs=P(None, "ga"), check_vma=False
    )
```

time: 484 us -> 95.3 us (0.20)
  waiting for transfers between devices: 356 us -> 0 us
  blocking collectives: 92.7 us -> 0 us
  Pallas kernels: 0 us -> 91.9 us
  matrix products: 16.2 us -> 0 us
  between operations: 13.5 us -> 0.01 us
    all_gather x1 -> x0, waiting for transfers between devices: 356 us -> none  [shards(): all_elements = lax.all_gather(flattened, 'ga', axis=1, tiled=True)]
    psum x1 -> x0, blocking collectives: 92.7 us -> none  [shards(): summed = lax.psum(matrix_flat, ('ga', 'ba'))]
    pallas_call x0 -> x1, Pallas kernels: none -> 91.9 us  [shards(): pl.pallas_call(kernel, out_shape=jax.ShapeDtypeStruct((2, 126), jnp.float...]
    dot_general x3 -> x0, matrix products: 16.2 us -> none  [the longest x1 14.3 us: shards(): jnp.dot(all_elements, screening, preferred_element_type=jnp.float32)]
  transfers between devices with their start and end apart: 1 -> 0, of which waited for: 1 -> 0; matrix products, arithmetic and copies ran while one was open for 0% -> 0% of each run, Pallas kernels for 0% -> 0%
where the time goes in v1:
time: 95.3 us; the launch traced here: 95.1 us
  Pallas kernels  91.9 us (96%)
  local copies, waits for them, and re-layouts  3.18 us (3%)
    pallas_call x1, Pallas kernels, shards(): pl.pallas_call(kernel, out_shape=jax.ShapeDtypeStruct((2, 126), jnp.float...  91.9 us
    unnamed x7, local copies, waits for them, and re-layouts  3.18 us

profile of v1, /device:TPU:1, one launch (start us, length us, event | category | flops | bytes accessed | tf_op | source)
XLA Modules:
  0.0 95.1 jit_solution(11941990793023315097)
XLA Ops:
  0.0 0.0 copy-start
  0.0 1.2 %copy-done = bf16[16,64,512]{2,1,0:T(8,128)(2,1)S(1)} copy-done((bf16[16,64,512]{2,1,0:T(8,128)(2,1)S(1)}, bf16[16,64,512]{2,1,0:T(8,128)(2,1)}, u32[]{:S(2)}) %copy-start) | copy-done | bytes 1048600
  1.2 0.0 copy-start.1
  1.2 0.7 copy-done.1
  1.9 0.0 copy-start.2
  1.9 0.7 copy-done.2
  2.6 91.9 %self_energy.1 = f32[2,126]{1,0:T(2,128)S(1)} custom-call(bf16[1024,512]{1,0:T(8,128)(2,1)S(1)} %bitcast.1, bf16[8192,512]{1,0:T(8,128)(2,1)} %w_ref.1, f32[2,16]{1,0:T(2,128)S(1)} %copy-done.2, s32[2,2016]{1,0:T(2,128)S(1)} %copy-done.1), custom_call_target="tpu_custom_call" | custom-call | flops 8999999488 | bytes 20971520 | tf_op jit(solution)/shard_map/self_energy/pallas_call | solution.py:235
  94.5 0.6 copy.6
Async XLA Ops:
  0.0 1.2 %copy-start = (bf16[16,64,512]{2,1,0:T(8,128)(2,1)S(1)}, bf16[16,64,512]{2,1,0:T(8,128)(2,1)}, u32[]{:S(2)}) copy-start(bf16[16,64,512]{2,1,0:T(8,128)(2,1)} %param.4) | copy-start | bytes 3145732
  1.2 0.7 copy-start.1
  1.9 0.7 copy-start.2

commit v2 on v1

v2 whole, which is shorter than its diff:
```python
import functools

import jax
import jax.numpy as jnp
from jax import lax
from jax.experimental import pallas as pl
from jax.experimental.pallas import tpu as pltpu
from jax.sharding import PartitionSpec as P

MESH = pl.DeviceIdType.MESH
GB = 512
CH = 128
NCH = 8
NBLK = 9
A0, A1, AM1, A2, AM2, B0, B2 = range(7)
UP1, UP2, DN1, DN2, X0, X2 = range(6)
NT = (((1,), (1,)), ((), ()))


def remote(src, dst, send, recv, device):
    return pltpu.make_async_remote_copy(
        src_ref=src, dst_ref=dst, send_sem=send, recv_sem=recv, device_id=device, device_id_type=MESH
    )


def wait_bytes(ref, sem):
    pltpu.make_async_copy(ref, ref, sem).wait()


def dot(a, b):
    return jnp.dot(a, b, preferred_element_type=jnp.float32)


def dot_nt(a, b):
    return lax.dot_general(a, b, NT, preferred_element_type=jnp.float32)


def halves(x):
    high = x.astype(jnp.bfloat16)
    return high, (x - high.astype(jnp.float32)).astype(jnp.bfloat16)


def kernel(
    m_ref, w_ref, bf_ref, pair_ref, out_ref,
    mv, wown, wf, t2, tm2, tb2, ab2, pairs, pp, one_n, facc, red_src, red_a, red_b,
    msend, mrecv, mloc, wloc, ploc, w1s, w1r, w2s, w2r, w3s, w3r, r1s, r1r, r2s, r2r,
):
    ga, ba = lax.axis_index("ga"), lax.axis_index("ba")
    z, s = ga // 2, lax.rem(ga, 2)
    y, xh, c = ba // 4, lax.rem(ba // 2, 2), lax.rem(ba, 2)

    def gai(dz, flip=0):
        side = 1 - s if flip else s
        return lax.rem(z + 8 + dz, 8) * 2 + side

    def bai(dy, dx, core):
        return (lax.rem(y + 4 + dy, 4) * 2 + lax.rem(xh + dx, 2)) * 2 + core

    def share(dy, dx, core):
        return (core * 4 + lax.rem(y + 4 + dy, 4)) * 2 + lax.rem(xh + dx, 2)

    barrier = pltpu.get_barrier_semaphore()

    @pl.loop(1, 16)
    def _(k):
        pl.semaphore_signal(barrier, inc=1, device_id=(lax.rem(ga + k, 16), ba), device_id_type=MESH)
        pl.semaphore_signal(barrier, inc=1, device_id=(ga, lax.rem(ba + k, 16)), device_id_type=MESH)

    own_p = pltpu.make_async_copy(pair_ref, pairs, ploc)
    own_p.start()
    own_m = pltpu.make_async_copy(m_ref, mv.at[A0], mloc)
    own_m.start()
    own_rows = (
        (A0, gai(0)), (A1, gai(1)), (AM1, gai(-1)), (A2, gai(2)), (AM2, gai(-2)),
        (B0, gai(0, 1)), (B2, gai(2, 1)),
    )
    own_w = []
    for slot, block in own_rows:
        cp = pltpu.make_async_copy(w_ref.at[pl.ds(block * GB, GB)], wown.at[slot], wloc.at[slot])
        cp.start()
        own_w.append(cp)

    pl.semaphore_wait(barrier, 30)

    mine_w = share(0, 0, c)
    plan = (
        (gai(2), ((gai(4), 6), (gai(4, 1), 7))),
        (gai(-2, 1), ((gai(-3, 1), 8),)),
        (gai(1), ((gai(3), 4), (gai(3, 1), 5))),
        (gai(-1), ((gai(-3), 3),)),
        (gai(0, 1), ((gai(-1, 1), 0), (gai(1, 1), 1), (gai(-2, 1), 2))),
    )
    for target, blocks in plan:
        for block, index in blocks:
            remote(
                w_ref.at[pl.ds(block * GB + mine_w * 32, 32)], wf.at[mine_w, index], w1s, w1r, (target, ba)
            ).start()

    def hop(flow, k):
        rows = pl.ds(pl.multiple_of(k * CH, CH), CH)
        src, dst, target = {
            UP1: (m_ref, AM1, gai(1)),
            DN1: (m_ref, A1, gai(-1)),
            UP2: (mv.at[AM1], AM2, gai(1)),
            DN2: (mv.at[A1], A2, gai(-1)),
            X0: (m_ref, B0, gai(0, 1)),
            X2: (mv.at[A2], B2, gai(0, 1)),
        }[flow]
        return remote(
            src.at[rows], mv.at[dst, rows], msend.at[flow, k], mrecv.at[flow, k], (target, ba)
        )

    @pl.loop(0, NCH)
    def _(k):
        hop(UP1, k).start()
        hop(DN1, k).start()
        hop(X0, k).start()

    own_p.wait()
    pp[...] = jnp.full(pp.shape, -1, jnp.int32)
    for a in range(16):
        pp[:, a * 128 : a * 128 + 126] = pairs[:, a * 126 : (a + 1) * 126]
    band = lax.rem(lax.broadcasted_iota(jnp.int32, (128, 2048), 0), 64)
    one_n[...] = jnp.where(band == pp[1:2, :], 1.0, 0.0).astype(jnp.bfloat16)
    facc[...] = jnp.zeros_like(facc)

    def pieces(index, first, count, sems, device):
        part = wf.at[pl.ds(first, count)]
        return remote(part, part, sems[0].at[index], sems[1].at[index], device)

    def arrived(index, first, count):
        part = wf.at[pl.ds(first, count)]
        remote(part, part, w2s.at[index], w2r.at[index], (ga, ba)).wait_recv()

    sems2, sems3 = (w2s, w2r), (w3s, w3r)
    other = (ga, bai(0, 0, 1 - c))
    up_y, down_y = (ga, bai(1, 0, c)), (ga, bai(-1, 0, c))
    base = (c * 4 + y) * 2
    base_up = (c * 4 + lax.rem(y + 1, 4)) * 2
    base_down = (c * 4 + lax.rem(y + 3, 4)) * 2
    base_far = (c * 4 + lax.rem(y + 2, 4)) * 2
    sends = []

    def launch(cp):
        cp.start()
        sends.append(cp)

    def fwd(k):
        hop(UP1, k).wait_recv()
        hop(UP2, k).start()
        hop(DN1, k).wait_recv()
        hop(DN2, k).start()

    lane = lax.broadcasted_iota(jnp.int32, (64, 128), 1) // 64

    def accumulate(per_band, first_band):
        for f in range(2):
            total = facc[pl.ds(f * 64, 64), :]
            for q in range(per_band.shape[0] // 64):
                part = per_band[q * 64 : (q + 1) * 64, (q // 2) * 128 : (q // 2 + 1) * 128]
                total += jnp.where(lane == q % 2, part * bf_ref[f, first_band + q], 0.0)
            facc[pl.ds(f * 64, 64), :] = total

    def by_column(applied, right):
        high, low = halves(applied)
        return dot_nt(high, right) + dot_nt(low, right)

    def by_row(left, turned):
        high, low = halves(turned)
        return dot(left, high) + dot(left, low)

    def block(index):
        return wf[:, index].reshape(GB, GB)

    def early(e):
        rows = pl.ds(pl.multiple_of(e * 256, 256), 256)
        hop(X0, 2 * e).wait_recv()
        hop(X0, 2 * e + 1).wait_recv()
        a0 = mv[A0, rows, :]
        applied = dot(a0, wown[A0])
        for slot in (A1, AM1, B0):
            applied += dot(mv[slot, rows, :], wown[slot])
        accumulate(by_column(applied, a0), 4 * e)
        t2[:, rows] = dot_nt(wown[A2], a0)
        tm2[:, rows] = dot_nt(wown[AM2], a0)
        tb2[:, rows] = dot_nt(wown[B2], a0)

    def middle(e):
        rows = pl.ds(pl.multiple_of(e * 256, 256), 256)
        am1, a1, b0 = mv[AM1, rows, :], mv[A1, rows, :], mv[B0, rows, :]
        accumulate(by_column(dot(am1, block(0)) + dot(a1, block(1)), b0), 4 * e)
        tm2[:, rows] += dot_nt(block(2), b0) + dot_nt(block(3), a1)
        t2[:, rows] += dot_nt(block(4), am1)
        tb2[:, rows] += dot_nt(block(5), am1)
        ab2[rows, :] = dot(am1, block(8))

    def late(k):
        rows = pl.ds(pl.multiple_of(k * CH, CH), CH)
        hop(UP2, k).wait_recv()
        am2 = mv[AM2, rows, :]
        tb2[:, rows] += dot_nt(block(7), am2)
        turned = t2[:, rows] + dot_nt(block(6), am2)
        accumulate(by_row(mv[A2, rows, :], turned) + by_row(am2, tm2[:, rows]), 2 * k)

    def last(k):
        rows = pl.ds(pl.multiple_of(k * CH, CH), CH)
        hop(X2, k).wait_recv()
        b2 = mv[B2, rows, :]
        accumulate(by_row(b2, tb2[:, rows]) + by_column(ab2[rows, :], b2), 2 * k)

    wait_bytes(wf.at[mine_w], w1r)
    launch(pieces(0, mine_w, 1, sems2, (ga, bai(0, 1, c))))
    fwd(0)
    arrived(0, share(0, 1, c), 1)
    launch(pieces(1, base, 2, sems2, up_y))
    launch(pieces(2, base, 2, sems2, down_y))
    launch(pieces(0, base, 2, sems3, other))
    fwd(1)
    own_m.wait()
    for cp in own_w:
        cp.wait()

    @pl.loop(0, 2)
    def _(e):
        fwd(2 * e + 2)
        fwd(2 * e + 3)
        early(e)

    arrived(1, base_down, 2)
    launch(pieces(3, base_down, 1, sems2, up_y))
    launch(pieces(1, base_down, 2, sems3, other))
    arrived(2, base_up, 2)
    launch(pieces(4, base_up + 1, 1, sems2, down_y))
    launch(pieces(2, base_up, 2, sems3, other))

    fwd(6)
    fwd(7)

    @pl.loop(2, 4)
    def _(e):
        early(e)

    arrived(3, base_far, 1)
    launch(pieces(3, base_far, 1, sems3, other))
    arrived(4, base_far + 1, 1)
    launch(pieces(4, base_far + 1, 1, sems3, other))
    mirror = (1 - 2 * c) * 8
    for index, first, count in (
        (0, base, 2), (1, base_down, 2), (2, base_up, 2), (3, base_far, 1), (4, base_far + 1, 1),
    ):
        part = wf.at[pl.ds(first + mirror, count)]
        remote(part, part, w3s.at[index], w3r.at[index], other).wait_recv()

    @pl.loop(0, NCH + 1)
    def _(k):
        @pl.when(k < NCH)
        def _():
            hop(DN2, k).wait_recv()
            hop(X2, k).start()

            @pl.when(lax.rem(k, 2) == 0)
            def _():
                middle(k // 2)

            late(k)

        @pl.when(k >= 1)
        def _():
            last(k - 1)

    full = facc[...]
    x1 = full.astype(jnp.bfloat16)
    rest = full - x1.astype(jnp.float32)
    x2 = rest.astype(jnp.bfloat16)
    x3 = (rest - x2.astype(jnp.float32)).astype(jnp.bfloat16)
    picked = (
        jnp.dot(x1, one_n[...], preferred_element_type=jnp.float32)
        + jnp.dot(x2, one_n[...], preferred_element_type=jnp.float32)
        + jnp.dot(x3, one_n[...], preferred_element_type=jnp.float32)
    )
    first = lax.broadcasted_iota(jnp.int32, (64, 2048), 0) == pp[0:1, :]
    for f in range(2):
        row = jnp.sum(jnp.where(first, picked[f * 64 : (f + 1) * 64], 0.0), axis=0, keepdims=True)
        for a in range(16):
            red_src[a, f : f + 1, :] = row[:, a * 128 : (a + 1) * 128]

    @pl.loop(1, 16)
    def _(k):
        peer = lax.rem(ga + k, 16)
        remote(red_src.at[peer], red_a.at[k - 1], r1s, r1r, (peer, ba)).start()

    wait_bytes(red_a, r1r)
    mine = red_src[ga]
    for k in range(15):
        mine += red_a[k]
    red_b[ba] = mine

    @pl.loop(1, 16)
    def _(k):
        peer = lax.rem(ba + k, 16)
        remote(red_b.at[ba], red_b.at[ba], r2s, r2r, (ga, peer)).start()

    wait_bytes(red_b.at[pl.ds(0, 15)], r2r)
    total = red_b[0]
    for k in range(1, 16):
        total += red_b[k]
    out_ref[...] = total[:, :126]

    wait_bytes(wf.at[0], w1s)
    for cp in sends:
        cp.wait_send()

    @pl.loop(0, NCH)
    def _(k):
        for flow in (UP1, DN1, UP2, DN2, X0, X2):
            hop(flow, k).wait_send()

    wait_bytes(red_a, r1s)
    wait_bytes(red_b.at[pl.ds(0, 15)], r2s)


def shards(matrix_elements, screening, band_factor, pair_list):
    bands, quasi, width = matrix_elements.shape
    dma = pltpu.SemaphoreType.DMA
    return pl.pallas_call(
        kernel,
        out_shape=jax.ShapeDtypeStruct((2, 126), jnp.float32),
        in_specs=[
            pl.BlockSpec(memory_space=pltpu.HBM),
            pl.BlockSpec(memory_space=pltpu.HBM),
            pl.BlockSpec(memory_space=pltpu.SMEM),
            pl.BlockSpec(memory_space=pltpu.HBM),
        ],
        out_specs=pl.BlockSpec(memory_space=pltpu.VMEM),
        scratch_shapes=[
            pltpu.VMEM((7, 1024, GB), jnp.bfloat16),
            pltpu.VMEM((7, GB, GB), jnp.bfloat16),
            pltpu.VMEM((16, NBLK, 32, GB), jnp.bfloat16),
            pltpu.VMEM((GB, 1024), jnp.float32),
            pltpu.VMEM((GB, 1024), jnp.float32),
            pltpu.VMEM((GB, 1024), jnp.float32),
            pltpu.VMEM((1024, GB), jnp.float32),
            pltpu.VMEM((2, 2016), jnp.int32),
            pltpu.VMEM((2, 2048), jnp.int32),
            pltpu.VMEM((128, 2048), jnp.bfloat16),
            pltpu.VMEM((128, 128), jnp.float32),
            pltpu.VMEM((16, 2, 128), jnp.float32),
            pltpu.VMEM((15, 2, 128), jnp.float32),
            pltpu.VMEM((16, 2, 128), jnp.float32),
            dma((6, NCH)), dma((6, NCH)), dma, dma((7,)), dma,
            dma, dma, dma((5,)), dma((5,)), dma((5,)), dma((5,)),
            dma, dma, dma, dma,
        ],
        compiler_params=pltpu.CompilerParams(
            collective_id=0, has_side_effects=True, vmem_limit_bytes=56 << 20
        ),
        cost_estimate=pl.CostEstimate(flops=9 * 10**9, bytes_accessed=20 << 20, transcendentals=0),
        name="self_energy",
    )(matrix_elements.reshape(bands * quasi, width), screening, band_factor, pair_list)


def solution(mesh):
    placed = (P("ba", None, "ga"), P(None, "ga"), P(None, "ba"), P())
    return jax.shard_map(
        shards, mesh=mesh, in_specs=placed, out_specs=P(None, "ga"), check_vma=False
    )
```

time: 95.3 us -> 107 us (1.12)
  Pallas kernels: 91.9 us -> 106 us
  local copies, waits for them, and re-layouts: 3.18 us -> 1.24 us
    pallas_call x1, Pallas kernels: 91.9 us -> 106 us  [shards(): pl.pallas_call(kernel, out_shape=jax.ShapeDtypeStruct((2, 126), jnp.float...]
    unnamed x7 -> x1, local copies, waits for them, and re-layouts: 3.18 us -> 1.24 us
where the time goes in v2:
time: 107 us
  Pallas kernels  106 us (99%)
  local copies, waits for them, and re-layouts  1.24 us (1%)
    pallas_call x1, Pallas kernels, shards(): pl.pallas_call(kernel, out_shape=jax.ShapeDtypeStruct((2, 126), jnp.float...  106 us

profile of v2, /device:TPU:1, one launch (start us, length us, event | category | flops | bytes accessed | tf_op | source)
XLA Modules:
  0.0 107.3 jit_solution(13851354318864293030)
XLA Ops:
  0.0 106.0 %self_energy.1 = f32[2,126]{1,0:T(2,128)} custom-call(bf16[1024,512]{1,0:T(8,128)(2,1)} %bitcast.1, bf16[8192,512]{1,0:T(8,128)(2,1)} %w_ref.1, f32[2,16]{1,0:T(2,128)} %bf_ref.1, s32[2,2016]{1,0:T(2,128)} %pair_ref.1), custom_call_target="tpu_custom_call" | custom-call | flops 8999999488 | bytes 20971520 | tf_op jit(solution)/shard_map/self_energy/pallas_call | solution.py:325
  106.0 1.2 %copy.6 = f32[2,126]{1,0:T(2,128)} copy(f32[2,126]{1,0:T(2,128)} %self_energy.1) | data formatting | bytes 2016

commit v3 on v2

--- a/solution.py
+++ b/solution.py
@@ -114,7 +114,6 @@
     def _(k):
         hop(UP1, k).start()
         hop(DN1, k).start()
-        hop(X0, k).start()
 
     own_p.wait()
     pp[...] = jnp.full(pp.shape, -1, jnp.int32)
@@ -210,6 +209,11 @@
 
     wait_bytes(wf.at[mine_w], w1r)
     launch(pieces(0, mine_w, 1, sems2, (ga, bai(0, 1, c))))
+
+    @pl.loop(0, NCH)
+    def _(k):
+        hop(X0, k).start()
+
     fwd(0)
     arrived(0, share(0, 1, c), 1)
     launch(pieces(1, base, 2, sems2, up_y))
@@ -236,10 +240,15 @@
     fwd(6)
     fwd(7)
 
-    @pl.loop(2, 4)
-    def _(e):
-        early(e)
-
+    def cross(k):
+        hop(DN2, k).wait_recv()
+        hop(X2, k).start()
+
+    cross(0)
+    early(2)
+    cross(1)
+    early(3)
+    cross(2)
     arrived(3, base_far, 1)
     launch(pieces(3, base_far, 1, sems3, other))
     arrived(4, base_far + 1, 1)
@@ -253,11 +262,12 @@
 
     @pl.loop(0, NCH + 1)
     def _(k):
+        @pl.when(k + 3 < NCH)
+        def _():
+            cross(k + 3)
+
         @pl.when(k < NCH)
         def _():
-            hop(DN2, k).wait_recv()
-            hop(X2, k).start()
-
             @pl.when(lax.rem(k, 2) == 0)
             def _():
                 middle(k // 2)

time: 107 us -> 85.3 us (0.80)
  Pallas kernels: 106 us -> 83.9 us
    pallas_call x1, Pallas kernels: 106 us -> 83.9 us  [shards(): pl.pallas_call(kernel, out_shape=jax.ShapeDtypeStruct((2, 126), jnp.float...]
where the time goes in v3:
time: 85.3 us; the launch traced here: 85.2 us
  Pallas kernels  83.9 us (98%)
  local copies, waits for them, and re-layouts  1.24 us (1%)
    pallas_call x1, Pallas kernels, shards(): pl.pallas_call(kernel, out_shape=jax.ShapeDtypeStruct((2, 126), jnp.float...  83.9 us

profile of v3, /device:TPU:1, one launch (start us, length us, event | category | flops | bytes accessed | tf_op | source)
XLA Modules:
  0.0 85.2 jit_solution(4494504382091401446)
XLA Ops:
  0.0 83.9 %self_energy.1 = f32[2,126]{1,0:T(2,128)} custom-call(bf16[1024,512]{1,0:T(8,128)(2,1)} %bitcast.1, bf16[8192,512]{1,0:T(8,128)(2,1)} %w_ref.1, f32[2,16]{1,0:T(2,128)} %bf_ref.1, s32[2,2016]{1,0:T(2,128)} %pair_ref.1), custom_call_target="tpu_custom_call" | custom-call | flops 8999999488 | bytes 20971520 | tf_op jit(solution)/shard_map/self_energy/pallas_call | solution.py:335
  83.9 1.2 %copy.6 = f32[2,126]{1,0:T(2,128)} copy(f32[2,126]{1,0:T(2,128)} %self_energy.1) | data formatting | bytes 2016

commit v4 on v2

--- a/solution.py
+++ b/solution.py
@@ -14,6 +14,7 @@
 NBLK = 9
 A0, A1, AM1, A2, AM2, B0, B2 = range(7)
 UP1, UP2, DN1, DN2, X0, X2 = range(6)
+FAR_FIRST = (8, 9, 7, 10, 6, 11, 5, 12, 4, 13, 3, 14, 2, 15, 1)
 NT = (((1,), (1,)), ((), ()))
 
 
@@ -55,9 +56,6 @@
 
     def bai(dy, dx, core):
         return (lax.rem(y + 4 + dy, 4) * 2 + lax.rem(xh + dx, 2)) * 2 + core
-
-    def share(dy, dx, core):
-        return (core * 4 + lax.rem(y + 4 + dy, 4)) * 2 + lax.rem(xh + dx, 2)
 
     barrier = pltpu.get_barrier_semaphore()
 
@@ -82,22 +80,25 @@
 
     pl.semaphore_wait(barrier, 30)
 
-    mine_w = share(0, 0, c)
+    here = c * 4 + y
     plan = (
+        (gai(0, 1), ((gai(-1, 1), 0), (gai(1, 1), 1), (gai(-2, 1), 2))),
+        (gai(-1), ((gai(-3), 3),)),
+        (gai(1), ((gai(3), 4), (gai(3, 1), 5))),
         (gai(2), ((gai(4), 6), (gai(4, 1), 7))),
         (gai(-2, 1), ((gai(-3, 1), 8),)),
-        (gai(1), ((gai(3), 4), (gai(3, 1), 5))),
-        (gai(-1), ((gai(-3), 3),)),
-        (gai(0, 1), ((gai(-1, 1), 0), (gai(1, 1), 1), (gai(-2, 1), 2))),
     )
     for target, blocks in plan:
         for block, index in blocks:
+            h = index // 5
             remote(
-                w_ref.at[pl.ds(block * GB + mine_w * 32, 32)], wf.at[mine_w, index], w1s, w1r, (target, ba)
+                w_ref.at[pl.ds(block * GB + here * 64, 64)], wf.at[here, index],
+                w1s.at[h], w1r.at[h], (target, ba),
             ).start()
 
     def hop(flow, k):
-        rows = pl.ds(pl.multiple_of(k * CH, CH), CH)
+        size = CH // 2 if flow in (DN2, X2) else CH
+        rows = pl.ds(pl.multiple_of(k * size, size), size)
         src, dst, target = {
             UP1: (m_ref, AM1, gai(1)),
             DN1: (m_ref, A1, gai(-1)),
@@ -124,32 +125,29 @@
     one_n[...] = jnp.where(band == pp[1:2, :], 1.0, 0.0).astype(jnp.bfloat16)
     facc[...] = jnp.zeros_like(facc)
 
-    def pieces(index, first, count, sems, device):
-        part = wf.at[pl.ds(first, count)]
-        return remote(part, part, sems[0].at[index], sems[1].at[index], device)
-
-    def arrived(index, first, count):
-        part = wf.at[pl.ds(first, count)]
-        remote(part, part, w2s.at[index], w2r.at[index], (ga, ba)).wait_recv()
-
-    sems2, sems3 = (w2s, w2r), (w3s, w3r)
-    other = (ga, bai(0, 0, 1 - c))
-    up_y, down_y = (ga, bai(1, 0, c)), (ga, bai(-1, 0, c))
-    base = (c * 4 + y) * 2
-    base_up = (c * 4 + lax.rem(y + 1, 4)) * 2
-    base_down = (c * 4 + lax.rem(y + 3, 4)) * 2
-    base_far = (c * 4 + lax.rem(y + 2, 4)) * 2
+    up, down, far = c * 4 + lax.rem(y + 1, 4), c * 4 + lax.rem(y + 3, 4), c * 4 + lax.rem(y + 2, 4)
+    up_y, down_y, other = (ga, bai(1, 0, c)), (ga, bai(-1, 0, c)), (ga, bai(0, 0, 1 - c))
+    part = (pl.ds(0, 5), pl.ds(5, 4))
     sends = []
 
     def launch(cp):
         cp.start()
         sends.append(cp)
+
+    def to_y(index, slot, h, device):
+        view = wf.at[slot, part[h]]
+        return remote(view, view, w2s.at[index], w2r.at[index], device)
+
+    def to_core(index, slot, h):
+        view = wf.at[slot, part[h]]
+        return remote(view, view, w3s.at[index], w3r.at[index], other)
 
     def fwd(k):
         hop(UP1, k).wait_recv()
         hop(UP2, k).start()
         hop(DN1, k).wait_recv()
-        hop(DN2, k).start()
+        hop(DN2, 2 * k).start()
+        hop(DN2, 2 * k + 1).start()
 
     lane = lax.broadcasted_iota(jnp.int32, (64, 128), 1) // 64
 
@@ -204,90 +202,106 @@
 
     def last(k):
         rows = pl.ds(pl.multiple_of(k * CH, CH), CH)
-        hop(X2, k).wait_recv()
+        hop(X2, 2 * k).wait_recv()
+        hop(X2, 2 * k + 1).wait_recv()
         b2 = mv[B2, rows, :]
         accumulate(by_row(b2, tb2[:, rows]) + by_column(ab2[rows, :], b2), 2 * k)
 
-    wait_bytes(wf.at[mine_w], w1r)
-    launch(pieces(0, mine_w, 1, sems2, (ga, bai(0, 1, c))))
+    def cross(k):
+        for h in range(2):
+            hop(DN2, 2 * k + h).wait_recv()
+            hop(X2, 2 * k + h).start()
+
+    def gather_own(h):
+        wait_bytes(wf.at[here, part[h]], w1r.at[h])
+        launch(to_y(h, here, h, up_y))
+        launch(to_y(2 + h, here, h, down_y))
+        launch(to_core(h, here, h))
+
+    def gather_near(h):
+        to_y(h, down, h, up_y).wait_recv()
+        if h == 0:
+            launch(to_y(4, down, h, up_y))
+        launch(to_core(2 + h, down, h))
+        to_y(2 + h, up, h, up_y).wait_recv()
+        if h == 1:
+            launch(to_y(5, up, h, down_y))
+        launch(to_core(4 + h, up, h))
+
+    gather_own(0)
     fwd(0)
-    arrived(0, share(0, 1, c), 1)
-    launch(pieces(1, base, 2, sems2, up_y))
-    launch(pieces(2, base, 2, sems2, down_y))
-    launch(pieces(0, base, 2, sems3, other))
+    gather_own(1)
     fwd(1)
     own_m.wait()
     for cp in own_w:
         cp.wait()
-
-    @pl.loop(0, 2)
-    def _(e):
-        fwd(2 * e + 2)
-        fwd(2 * e + 3)
-        early(e)
-
-    arrived(1, base_down, 2)
-    launch(pieces(3, base_down, 1, sems2, up_y))
-    launch(pieces(1, base_down, 2, sems3, other))
-    arrived(2, base_up, 2)
-    launch(pieces(4, base_up + 1, 1, sems2, down_y))
-    launch(pieces(2, base_up, 2, sems3, other))
-
+    gather_near(0)
+    fwd(2)
+    fwd(3)
+    early(0)
+    gather_near(1)
+    fwd(4)
+    fwd(5)
+    early(1)
+    to_y(4, far, 0, up_y).wait_recv()
+    launch(to_core(6, far, 0))
     fwd(6)
     fwd(7)
-
-    @pl.loop(2, 4)
-    def _(e):
-        early(e)
-
-    arrived(3, base_far, 1)
-    launch(pieces(3, base_far, 1, sems3, other))
-    arrived(4, base_far + 1, 1)
-    launch(pieces(4, base_far + 1, 1, sems3, other))
-    mirror = (1 - 2 * c) * 8
-    for index, first, count in (
-        (0, base, 2), (1, base_down, 2), (2, base_up, 2), (3, base_far, 1), (4, base_far + 1, 1),
-    ):
-        part = wf.at[pl.ds(first + mirror, count)]
-        remote(part, part, w3s.at[index], w3r.at[index], other).wait_recv()
+    early(2)
+    to_y(5, far, 1, up_y).wait_recv()
+    launch(to_core(7, far, 1))
+    cross(0)
+    early(3)
+    cross(1)
+    mirror = (1 - 2 * c) * 4
+    for index, slot in enumerate((here, here, down, down, up, up, far, far)):
+        to_core(index, slot + mirror, index % 2).wait_recv()
 
     @pl.loop(0, NCH + 1)
     def _(k):
-        @pl.when(k < NCH)
+        @pl.when(k + 2 < NCH)
         def _():
-            hop(DN2, k).wait_recv()
-            hop(X2, k).start()
-
-            @pl.when(lax.rem(k, 2) == 0)
-            def _():
-                middle(k // 2)
-
-            late(k)
+            cross(k + 2)
 
         @pl.when(k >= 1)
         def _():
             last(k - 1)
+
+        @pl.when(k < NCH // 2)
+        def _():
+            middle(k)
+
+        @pl.when(k < NCH)
+        def _():
+            late(k)
 
     full = facc[...]
     x1 = full.astype(jnp.bfloat16)
     rest = full - x1.astype(jnp.float32)
     x2 = rest.astype(jnp.bfloat16)
-    x3 = (rest - x2.astype(jnp.float32)).astype(jnp.bfloat16)
-    picked = (
-        jnp.dot(x1, one_n[...], preferred_element_type=jnp.float32)
-        + jnp.dot(x2, one_n[...], preferred_element_type=jnp.float32)
-        + jnp.dot(x3, one_n[...], preferred_element_type=jnp.float32)
-    )
+    picked = dot(x1, one_n[...]) + dot(x2, one_n[...])
     first = lax.broadcasted_iota(jnp.int32, (64, 2048), 0) == pp[0:1, :]
     for f in range(2):
         row = jnp.sum(jnp.where(first, picked[f * 64 : (f + 1) * 64], 0.0), axis=0, keepdims=True)
         for a in range(16):
             red_src[a, f : f + 1, :] = row[:, a * 128 : (a + 1) * 128]
 
-    @pl.loop(1, 16)
-    def _(k):
+    for k in FAR_FIRST:
         peer = lax.rem(ga + k, 16)
         remote(red_src.at[peer], red_a.at[k - 1], r1s, r1r, (peer, ba)).start()
+
+    for h in range(2):
+        wait_bytes(wf.at[here, part[h]], w1s.at[h])
+    for cp in sends:
+        cp.wait_send()
+
+    @pl.loop(0, NCH)
+    def _(k):
+        for flow in (UP1, DN1, UP2, X0):
+            hop(flow, k).wait_send()
+        for flow in (DN2, X2):
+            hop(flow, 2 * k).wait_send()
+            hop(flow, 2 * k + 1).wait_send()
 
     wait_bytes(red_a, r1r)
     mine = red_src[ga]
@@ -295,27 +309,17 @@
         mine += red_a[k]
     red_b[ba] = mine
 
-    @pl.loop(1, 16)
-    def _(k):
+    for k in FAR_FIRST:
         peer = lax.rem(ba + k, 16)
         remote(red_b.at[ba], red_b.at[ba], r2s, r2r, (ga, peer)).start()
 
+    wait_bytes(red_a, r1s)
     wait_bytes(red_b.at[pl.ds(0, 15)], r2r)
     total = red_b[0]
     for k in range(1, 16):
         total += red_b[k]
     out_ref[...] = total[:, :126]
 
-    wait_bytes(wf.at[0], w1s)
-    for cp in sends:
-        cp.wait_send()
-
-    @pl.loop(0, NCH)
-    def _(k):
-        for flow in (UP1, DN1, UP2, DN2, X0, X2):
-            hop(flow, k).wait_send()
-
-    wait_bytes(red_a, r1s)
     wait_bytes(red_b.at[pl.ds(0, 15)], r2s)
 
 
@@ -335,7 +339,7 @@
         scratch_shapes=[
             pltpu.VMEM((7, 1024, GB), jnp.bfloat16),
             pltpu.VMEM((7, GB, GB), jnp.bfloat16),
-            pltpu.VMEM((16, NBLK, 32, GB), jnp.bfloat16),
+            pltpu.VMEM((8, NBLK, 64, GB), jnp.bfloat16),
             pltpu.VMEM((GB, 1024), jnp.float32),
             pltpu.VMEM((GB, 1024), jnp.float32),
             pltpu.VMEM((GB, 1024), jnp.float32),
@@ -347,12 +351,12 @@
             pltpu.VMEM((16, 2, 128), jnp.float32),
             pltpu.VMEM((15, 2, 128), jnp.float32),
             pltpu.VMEM((16, 2, 128), jnp.float32),
-            dma((6, NCH)), dma((6, NCH)), dma, dma((7,)), dma,
-            dma, dma, dma((5,)), dma((5,)), dma((5,)), dma((5,)),
+            dma((6, 2 * NCH)), dma((6, 2 * NCH)), dma, dma((7,)), dma,
+            dma((2,)), dma((2,)), dma((6,)), dma((6,)), dma((8,)), dma((8,)),
             dma, dma, dma, dma,
         ],
         compiler_params=pltpu.CompilerParams(
-            collective_id=0, has_side_effects=True, vmem_limit_bytes=56 << 20
+            collective_id=0, has_side_effects=True, vmem_limit_bytes=44 << 20
         ),
         cost_estimate=pl.CostEstimate(flops=9 * 10**9, bytes_accessed=20 << 20, transcendentals=0),
         name="self_energy",

time: 107 us -> 89 us (0.83)
  Pallas kernels: 106 us -> 82.3 us
  local copies, waits for them, and re-layouts: 1.24 us -> 6.57 us
    pallas_call x1, Pallas kernels: 106 us -> 82.3 us  [shards(): pl.pallas_call(kernel, out_shape=jax.ShapeDtypeStruct((2, 126), jnp.float...]
    unnamed x1 -> x9, local copies, waits for them, and re-layouts: 1.24 us -> 6.57 us
where the time goes in v4:
time: 89 us; the launch traced here: 88.8 us
  Pallas kernels  82.3 us (92%)
  local copies, waits for them, and re-layouts  6.57 us (7%)
    pallas_call x1, Pallas kernels, shards(): pl.pallas_call(kernel, out_shape=jax.ShapeDtypeStruct((2, 126), jnp.float...  82.3 us
    unnamed x9, local copies, waits for them, and re-layouts  6.57 us

profile of v4, /device:TPU:1, one launch (start us, length us, event | category | flops | bytes accessed | tf_op | source)
XLA Modules:
  0.0 88.8 jit_solution(10187728408447330460)
XLA Ops:
  0.0 0.0 copy-start
  0.0 3.4 %copy-done = bf16[8192,512]{1,0:T(8,128)(2,1)S(1)} copy-done((bf16[8192,512]{1,0:T(8,128)(2,1)S(1)}, bf16[8192,512]{1,0:T(8,128)(2,1)}, u32[]{:S(2)}) %copy-start) | copy-done | bytes 8388632
  3.4 0.0 copy-start.1
  3.4 1.2 %copy-done.1 = bf16[16,64,512]{2,1,0:T(8,128)(2,1)S(1)} copy-done((bf16[16,64,512]{2,1,0:T(8,128)(2,1)S(1)}, bf16[16,64,512]{2,1,0:T(8,128)(2,1)}, u32[]{:S(2)}) %copy-start.1) | copy-done | bytes 1048600
  4.6 0.0 copy-start.2
  4.6 0.7 copy-done.2
  5.3 0.0 copy-start.3
  5.3 0.7 copy-done.3
  6.0 82.3 %self_energy.1 = f32[2,126]{1,0:T(2,128)S(1)} custom-call(bf16[1024,512]{1,0:T(8,128)(2,1)S(1)} %bitcast.1, bf16[8192,512]{1,0:T(8,128)(2,1)S(1)} %copy-done, f32[2,16]{1,0:T(2,128)S(1)} %copy-done.3, s32[2,2016]{1,0:T(2,128)S(1)} %copy-done.2), custom_call_target="tpu_custom_call" | custom-call | flops 8999999488 | bytes 20971520 | tf_op jit(solution)/shard_map/self_energy/pallas_call | solution.py:329
  88.3 0.6 copy.6
Async XLA Ops:
  0.0 3.4 %copy-start = (bf16[8192,512]{1,0:T(8,128)(2,1)S(1)}, bf16[8192,512]{1,0:T(8,128)(2,1)}, u32[]{:S(2)}) copy-start(bf16[8192,512]{1,0:T(8,128)(2,1)} %w_ref.1) | copy-start | bytes 25165828
  3.4 1.2 %copy-start.1 = (bf16[16,64,512]{2,1,0:T(8,128)(2,1)S(1)}, bf16[16,64,512]{2,1,0:T(8,128)(2,1)}, u32[]{:S(2)}) copy-start(bf16[16,64,512]{2,1,0:T(8,128)(2,1)} %param.4) | copy-start | bytes 3145732
  4.6 0.7 copy-start.2
  5.3 0.7 copy-start.3

commit v5 on v4

--- a/solution.py
+++ b/solution.py
@@ -44,7 +44,7 @@
 def kernel(
     m_ref, w_ref, bf_ref, pair_ref, out_ref,
     mv, wown, wf, t2, tm2, tb2, ab2, pairs, pp, one_n, facc, red_src, red_a, red_b,
-    msend, mrecv, mloc, wloc, ploc, w1s, w1r, w2s, w2r, w3s, w3r, r1s, r1r, r2s, r2r,
+    msend, mrecv, mloc, wloc, ploc, known, w1s, w1r, w2s, w2r, w3s, w3r, r1s, r1r, r2s, r2r,
 ):
     ga, ba = lax.axis_index("ga"), lax.axis_index("ba")
     z, s = ga // 2, lax.rem(ga, 2)
@@ -59,10 +59,16 @@
 
     barrier = pltpu.get_barrier_semaphore()
 
-    @pl.loop(1, 16)
-    def _(k):
-        pl.semaphore_signal(barrier, inc=1, device_id=(lax.rem(ga + k, 16), ba), device_id_type=MESH)
-        pl.semaphore_signal(barrier, inc=1, device_id=(ga, lax.rem(ba + k, 16)), device_id_type=MESH)
+    neighbours = (
+        (gai(1), ba), (gai(-1), ba), (gai(0, 1), ba), (gai(0, 1), bai(0, 1, c)),
+        (ga, bai(1, 0, c)), (ga, bai(-1, 0, c)), (ga, bai(0, 0, 1 - c)),
+    )
+
+    def greet(sem):
+        for device in neighbours:
+            pl.semaphore_signal(sem, inc=1, device_id=device, device_id_type=MESH)
+
+    greet(barrier)
 
     own_p = pltpu.make_async_copy(pair_ref, pairs, ploc)
     own_p.start()
@@ -77,24 +83,6 @@
         cp = pltpu.make_async_copy(w_ref.at[pl.ds(block * GB, GB)], wown.at[slot], wloc.at[slot])
         cp.start()
         own_w.append(cp)
-
-    pl.semaphore_wait(barrier, 30)
-
-    here = c * 4 + y
-    plan = (
-        (gai(0, 1), ((gai(-1, 1), 0), (gai(1, 1), 1), (gai(-2, 1), 2))),
-        (gai(-1), ((gai(-3), 3),)),
-        (gai(1), ((gai(3), 4), (gai(3, 1), 5))),
-        (gai(2), ((gai(4), 6), (gai(4, 1), 7))),
-        (gai(-2, 1), ((gai(-3, 1), 8),)),
-    )
-    for target, blocks in plan:
-        for block, index in blocks:
-            h = index // 5
-            remote(
-                w_ref.at[pl.ds(block * GB + here * 64, 64)], wf.at[here, index],
-                w1s.at[h], w1r.at[h], (target, ba),
-            ).start()
 
     def hop(flow, k):
         size = CH // 2 if flow in (DN2, X2) else CH
@@ -111,11 +99,38 @@
             src.at[rows], mv.at[dst, rows], msend.at[flow, k], mrecv.at[flow, k], (target, ba)
         )
 
-    @pl.loop(0, NCH)
-    def _(k):
+    def first(k):
         hop(UP1, k).start()
         hop(DN1, k).start()
         hop(X0, k).start()
+
+    here = c * 4 + y
+
+    def give(target, *blocks):
+        for block, index in blocks:
+            h = index // 5
+            remote(
+                w_ref.at[pl.ds(block * GB + here * 64, 64)], wf.at[here, index],
+                w1s.at[h], w1r.at[h], (target, ba),
+            ).start()
+
+    pl.semaphore_wait(barrier, 7)
+    greet(known.at[0])
+    first(0)
+    give(gai(0, 1), (gai(-1, 1), 0), (gai(1, 1), 1), (gai(-2, 1), 2))
+    give(gai(-1), (gai(-3), 3))
+    give(gai(1), (gai(3), 4), (gai(3, 1), 5))
+    pl.semaphore_wait(known.at[0], 7)
+    greet(known.at[1])
+    give(gai(2), (gai(4), 6), (gai(4, 1), 7))
+    first(1)
+    pl.semaphore_wait(known.at[1], 7)
+    greet(known.at[2])
+    give(gai(-2, 1), (gai(-3, 1), 8))
+
+    @pl.loop(2, NCH)
+    def _(k):
+        first(k)
 
     own_p.wait()
     pp[...] = jnp.full(pp.shape, -1, jnp.int32)
@@ -124,6 +139,8 @@
     band = lax.rem(lax.broadcasted_iota(jnp.int32, (128, 2048), 0), 64)
     one_n[...] = jnp.where(band == pp[1:2, :], 1.0, 0.0).astype(jnp.bfloat16)
     facc[...] = jnp.zeros_like(facc)
+    pl.semaphore_wait(known.at[2], 7)
+    greet(known.at[3])
 
     up, down, far = c * 4 + lax.rem(y + 1, 4), c * 4 + lax.rem(y + 3, 4), c * 4 + lax.rem(y + 2, 4)
     up_y, down_y, other = (ga, bai(1, 0, c)), (ga, bai(-1, 0, c)), (ga, bai(0, 0, 1 - c))
@@ -232,6 +249,7 @@
     fwd(0)
     gather_own(1)
     fwd(1)
+    pl.semaphore_wait(known.at[3], 7)
     own_m.wait()
     for cp in own_w:
         cp.wait()
@@ -280,9 +298,9 @@
     rest = full - x1.astype(jnp.float32)
     x2 = rest.astype(jnp.bfloat16)
     picked = dot(x1, one_n[...]) + dot(x2, one_n[...])
-    first = lax.broadcasted_iota(jnp.int32, (64, 2048), 0) == pp[0:1, :]
+    one_m = lax.broadcasted_iota(jnp.int32, (64, 2048), 0) == pp[0:1, :]
     for f in range(2):
-        row = jnp.sum(jnp.where(first, picked[f * 64 : (f + 1) * 64], 0.0), axis=0, keepdims=True)
+        row = jnp.sum(jnp.where(one_m, picked[f * 64 : (f + 1) * 64], 0.0), axis=0, keepdims=True)
         for a in range(16):
             red_src[a, f : f + 1, :] = row[:, a * 128 : (a + 1) * 128]
 
@@ -352,11 +370,11 @@
             pltpu.VMEM((15, 2, 128), jnp.float32),
             pltpu.VMEM((16, 2, 128), jnp.float32),
             dma((6, 2 * NCH)), dma((6, 2 * NCH)), dma, dma((7,)), dma,
-            dma((2,)), dma((2,)), dma((6,)), dma((6,)), dma((8,)), dma((8,)),
+            pltpu.SemaphoreType.REGULAR((4,)), dma((2,)), dma((2,)), dma((6,)), dma((6,)), dma((8,)), dma((8,)),
             dma, dma, dma, dma,
         ],
         compiler_params=pltpu.CompilerParams(
-            collective_id=0, has_side_effects=True, vmem_limit_bytes=44 << 20
+            collective_id=0, has_side_effects=True, vmem_limit_bytes=56 << 20
         ),
         cost_estimate=pl.CostEstimate(flops=9 * 10**9, bytes_accessed=20 << 20, transcendentals=0),
         name="self_energy",

time: 89 us -> 82.5 us (0.927)
  local copies, waits for them, and re-layouts: 6.57 us -> 1.24 us
  Pallas kernels: 82.3 us -> 81.1 us
    unnamed x9 -> x1, local copies, waits for them, and re-layouts: 6.57 us -> 1.24 us
    pallas_call x1, Pallas kernels: 82.3 us -> 81.1 us  [shards(): pl.pallas_call(kernel, out_shape=jax.ShapeDtypeStruct((2, 126), jnp.float...]
where the time goes in v5:
time: 82.5 us; the launch traced here: 82.3 us
  Pallas kernels  81.1 us (98%)
  local copies, waits for them, and re-layouts  1.24 us (2%)
    pallas_call x1, Pallas kernels, shards(): pl.pallas_call(kernel, out_shape=jax.ShapeDtypeStruct((2, 126), jnp.float...  81.1 us

profile of v5, /device:TPU:1, one launch (start us, length us, event | category | flops | bytes accessed | tf_op | source)
XLA Modules:
  0.0 82.3 jit_solution(14746056597294279506)
XLA Ops:
  0.0 81.1 %self_energy.1 = f32[2,126]{1,0:T(2,128)} custom-call(bf16[1024,512]{1,0:T(8,128)(2,1)} %bitcast.1, bf16[8192,512]{1,0:T(8,128)(2,1)} %w_ref.1, f32[2,16]{1,0:T(2,128)} %bf_ref.1, s32[2,2016]{1,0:T(2,128)} %pair_ref.1), custom_call_target="tpu_custom_call" | custom-call | flops 8999999488 | bytes 20971520 | tf_op jit(solution)/shard_map/self_energy/pallas_call | solution.py:347
  81.1 1.2 %copy.6 = f32[2,126]{1,0:T(2,128)} copy(f32[2,126]{1,0:T(2,128)} %self_energy.1) | data formatting | bytes 2016

commit v6 on v5

--- a/solution.py
+++ b/solution.py
@@ -11,7 +11,8 @@
 GB = 512
 CH = 128
 NCH = 8
-NBLK = 9
+NEAR = 3
+FAR = 6
 A0, A1, AM1, A2, AM2, B0, B2 = range(7)
 UP1, UP2, DN1, DN2, X0, X2 = range(6)
 FAR_FIRST = (8, 9, 7, 10, 6, 11, 5, 12, 4, 13, 3, 14, 2, 15, 1)
@@ -43,8 +44,8 @@
 
 def kernel(
     m_ref, w_ref, bf_ref, pair_ref, out_ref,
-    mv, wown, wf, t2, tm2, tb2, ab2, pairs, pp, one_n, facc, red_src, red_a, red_b,
-    msend, mrecv, mloc, wloc, ploc, known, w1s, w1r, w2s, w2r, w3s, w3r, r1s, r1r, r2s, r2r,
+    mv, wown, wn, wd, stage, t2, tm2, tb2, ab2, pairs, pp, one_n, facc, red_src, red_a, red_b,
+    msend, mrecv, mloc, wloc, ploc, known, w1s, w1r, xs, xr, w2s, w2r, w3s, w3r, r1s, r1r, r2s, r2r,
 ):
     ga, ba = lax.axis_index("ga"), lax.axis_index("ba")
     z, s = ga // 2, lax.rem(ga, 2)
@@ -102,34 +103,43 @@
     def first(k):
         hop(UP1, k).start()
         hop(DN1, k).start()
-        hop(X0, k).start()
+        if k < 5:
+            hop(X0, k).start()
 
     here = c * 4 + y
-
-    def give(target, *blocks):
-        for block, index in blocks:
-            h = index // 5
-            remote(
-                w_ref.at[pl.ds(block * GB + here * 64, 64)], wf.at[here, index],
-                w1s.at[h], w1r.at[h], (target, ba),
-            ).start()
+    same, swap = xh, 1 - xh
+    beyond = (gai(0, 1), bai(0, 1, c))
+
+    def give_near(block, index):
+        remote(
+            w_ref.at[pl.ds(block * GB + here * 64, 64)], wn.at[here, index], w1s.at[0], w1r.at[0], beyond
+        ).start()
+
+    def give_far(device, piece, block, index):
+        remote(
+            w_ref.at[pl.ds(block * GB + piece * 32, 32)], wd.at[piece, index], w1s.at[1], w1r.at[1], device
+        ).start()
 
     pl.semaphore_wait(barrier, 7)
     greet(known.at[0])
     first(0)
-    give(gai(0, 1), (gai(-1, 1), 0), (gai(1, 1), 1), (gai(-2, 1), 2))
-    give(gai(-1), (gai(-3), 3))
-    give(gai(1), (gai(3), 4), (gai(3, 1), 5))
+    own = here * 2 + same
+    give_near(gai(-1, 1), 0)
+    give_near(gai(1, 1), 1)
+    give_near(gai(-2, 1), 2)
+    give_far((gai(-1), ba), own, gai(-3), 0)
+    give_far((gai(1), ba), own, gai(3), 1)
+    give_far((gai(1), ba), own, gai(3, 1), 2)
+    first(1)
+    first(2)
     pl.semaphore_wait(known.at[0], 7)
     greet(known.at[1])
-    give(gai(2), (gai(4), 6), (gai(4, 1), 7))
-    first(1)
+    give_far((gai(2), ba), own, gai(4), 3)
+    give_far((gai(2), ba), own, gai(4, 1), 4)
     pl.semaphore_wait(known.at[1], 7)
     greet(known.at[2])
-    give(gai(-2, 1), (gai(-3, 1), 8))
-
-    @pl.loop(2, NCH)
-    def _(k):
+    give_far((gai(-2, 1), bai(0, 1, c)), here * 2 + swap, gai(-3, 1), 5)
+    for k in range(3, NCH):
         first(k)
 
     own_p.wait()
@@ -142,22 +152,29 @@
     pl.semaphore_wait(known.at[2], 7)
     greet(known.at[3])
 
-    up, down, far = c * 4 + lax.rem(y + 1, 4), c * 4 + lax.rem(y + 3, 4), c * 4 + lax.rem(y + 2, 4)
+    up, down, over = c * 4 + lax.rem(y + 1, 4), c * 4 + lax.rem(y + 3, 4), c * 4 + lax.rem(y + 2, 4)
     up_y, down_y, other = (ga, bai(1, 0, c)), (ga, bai(-1, 0, c)), (ga, bai(0, 0, 1 - c))
-    part = (pl.ds(0, 5), pl.ds(5, 4))
     sends = []
 
     def launch(cp):
         cp.start()
         sends.append(cp)
 
-    def to_y(index, slot, h, device):
-        view = wf.at[slot, part[h]]
+    def to_y(index, view, device):
         return remote(view, view, w2s.at[index], w2r.at[index], device)
 
-    def to_core(index, slot, h):
-        view = wf.at[slot, part[h]]
+    def to_core(index, view):
         return remote(view, view, w3s.at[index], w3r.at[index], other)
+
+    def x_first(h):
+        part = pl.ds(3 * h, 3)
+        return remote(wd.at[own, part], stage.at[part], xs.at[h], xr.at[h], beyond)
+
+    def x_second(h):
+        part = pl.ds(3 * h, 3)
+        return remote(
+            stage.at[part], wd.at[here * 2 + swap, part], xs.at[2 + h], xr.at[2 + h], (gai(0, 1), ba)
+        )
 
     def fwd(k):
         hop(UP1, k).wait_recv()
@@ -185,7 +202,9 @@
         return dot(left, high) + dot(left, low)
 
     def block(index):
-        return wf[:, index].reshape(GB, GB)
+        if index < NEAR:
+            return wn[:, index].reshape(GB, GB)
+        return wd[:, index - NEAR].reshape(GB, GB)
 
     def early(e):
         rows = pl.ds(pl.multiple_of(e * 256, 256), 256)
@@ -200,27 +219,33 @@
         tm2[:, rows] = dot_nt(wown[AM2], a0)
         tb2[:, rows] = dot_nt(wown[B2], a0)
 
-    def middle(e):
+    def near(e):
         rows = pl.ds(pl.multiple_of(e * 256, 256), 256)
         am1, a1, b0 = mv[AM1, rows, :], mv[A1, rows, :], mv[B0, rows, :]
         accumulate(by_column(dot(am1, block(0)) + dot(a1, block(1)), b0), 4 * e)
-        tm2[:, rows] += dot_nt(block(2), b0) + dot_nt(block(3), a1)
+        tm2[:, rows] += dot_nt(block(2), b0)
+
+    def middle(e):
+        rows = pl.ds(pl.multiple_of(e * 256, 256), 256)
+        am1, a1 = mv[AM1, rows, :], mv[A1, rows, :]
+        tm2[:, rows] += dot_nt(block(3), a1)
         t2[:, rows] += dot_nt(block(4), am1)
         tb2[:, rows] += dot_nt(block(5), am1)
         ab2[rows, :] = dot(am1, block(8))
 
-    def late(k):
-        rows = pl.ds(pl.multiple_of(k * CH, CH), CH)
-        hop(UP2, k).wait_recv()
+    def late(k, count=1):
+        rows = pl.ds(k * CH, count * CH)
+        for j in range(count):
+            hop(UP2, k + j).wait_recv()
         am2 = mv[AM2, rows, :]
         tb2[:, rows] += dot_nt(block(7), am2)
         turned = t2[:, rows] + dot_nt(block(6), am2)
         accumulate(by_row(mv[A2, rows, :], turned) + by_row(am2, tm2[:, rows]), 2 * k)
 
-    def last(k):
-        rows = pl.ds(pl.multiple_of(k * CH, CH), CH)
-        hop(X2, 2 * k).wait_recv()
-        hop(X2, 2 * k + 1).wait_recv()
+    def last(k, count=1):
+        rows = pl.ds(k * CH, count * CH)
+        for j in range(2 * count):
+            hop(X2, 2 * k + j).wait_recv()
         b2 = mv[B2, rows, :]
         accumulate(by_row(b2, tb2[:, rows]) + by_column(ab2[rows, :], b2), 2 * k)
 
@@ -229,69 +254,99 @@
             hop(DN2, 2 * k + h).wait_recv()
             hop(X2, 2 * k + h).start()
 
-    def gather_own(h):
-        wait_bytes(wf.at[here, part[h]], w1r.at[h])
-        launch(to_y(h, here, h, up_y))
-        launch(to_y(2 + h, here, h, down_y))
-        launch(to_core(h, here, h))
-
-    def gather_near(h):
-        to_y(h, down, h, up_y).wait_recv()
-        if h == 0:
-            launch(to_y(4, down, h, up_y))
-        launch(to_core(2 + h, down, h))
-        to_y(2 + h, up, h, up_y).wait_recv()
-        if h == 1:
-            launch(to_y(5, up, h, down_y))
-        launch(to_core(4 + h, up, h))
-
-    gather_own(0)
+    wait_bytes(wn.at[here], w1r.at[0])
+    launch(to_y(0, wn.at[here], up_y))
+    launch(to_y(1, wn.at[here], down_y))
+    launch(to_core(0, wn.at[here]))
     fwd(0)
-    gather_own(1)
     fwd(1)
-    pl.semaphore_wait(known.at[3], 7)
+    wait_bytes(wd.at[own], w1r.at[1])
+    launch(x_first(0))
+    launch(x_first(1))
+    launch(to_y(3, wd.at[own], up_y))
+    launch(to_y(4, wd.at[own], down_y))
+    launch(to_core(4, wd.at[own]))
+    fwd(2)
+    hop(X0, 5).start()
+    to_y(0, wn.at[down], up_y).wait_recv()
+    launch(to_y(2, wn.at[down], up_y))
+    launch(to_core(1, wn.at[down]))
+    to_y(1, wn.at[up], up_y).wait_recv()
+    launch(to_core(2, wn.at[up]))
+    fwd(3)
+    for h in range(2):
+        x_first(h).wait_recv()
+        launch(x_second(h))
+    fwd(4)
+    hop(X0, 6).start()
+    hop(X0, 7).start()
     own_m.wait()
     for cp in own_w:
         cp.wait()
-    gather_near(0)
-    fwd(2)
-    fwd(3)
     early(0)
-    gather_near(1)
-    fwd(4)
+    to_y(3, wd.at[down * 2 + same], up_y).wait_recv()
+    launch(to_y(7, wd.at[down * 2 + same], up_y))
+    launch(to_core(5, wd.at[down * 2 + same]))
+    to_y(4, wd.at[up * 2 + same], up_y).wait_recv()
+    launch(to_core(6, wd.at[up * 2 + same]))
     fwd(5)
     early(1)
-    to_y(4, far, 0, up_y).wait_recv()
-    launch(to_core(6, far, 0))
+    to_y(2, wn.at[over], up_y).wait_recv()
+    launch(to_core(3, wn.at[over]))
     fwd(6)
+    mirror = (1 - 2 * c) * 4
+    for index, slot in enumerate((here, down, up, over)):
+        to_core(index, wn.at[slot + mirror]).wait_recv()
+    near(0)
     fwd(7)
+    x_second(0).wait_recv()
+    x_second(1).wait_recv()
+    launch(to_y(5, wd.at[here * 2 + swap], up_y))
+    launch(to_y(6, wd.at[here * 2 + swap], down_y))
+    launch(to_core(7, wd.at[here * 2 + swap]))
+    to_y(7, wd.at[over * 2 + same], up_y).wait_recv()
+    launch(to_core(8, wd.at[over * 2 + same]))
+    near(1)
+    cross(0)
     early(2)
-    to_y(5, far, 1, up_y).wait_recv()
-    launch(to_core(7, far, 1))
-    cross(0)
+    cross(1)
+    to_y(6, wd.at[up * 2 + swap], up_y).wait_recv()
+    launch(to_y(8, wd.at[up * 2 + swap], down_y))
+    launch(to_core(9, wd.at[up * 2 + swap]))
+    to_y(5, wd.at[down * 2 + swap], up_y).wait_recv()
+    launch(to_core(10, wd.at[down * 2 + swap]))
+    near(2)
+    cross(2)
+    pl.semaphore_wait(known.at[3], 7)
     early(3)
-    cross(1)
-    mirror = (1 - 2 * c) * 4
-    for index, slot in enumerate((here, here, down, down, up, up, far, far)):
-        to_core(index, slot + mirror, index % 2).wait_recv()
-
-    @pl.loop(0, NCH + 1)
-    def _(k):
-        @pl.when(k + 2 < NCH)
-        def _():
-            cross(k + 2)
-
-        @pl.when(k >= 1)
-        def _():
-            last(k - 1)
-
-        @pl.when(k < NCH // 2)
-        def _():
-            middle(k)
-
-        @pl.when(k < NCH)
-        def _():
-            late(k)
+    cross(3)
+    near(3)
+    to_y(8, wd.at[over * 2 + swap], up_y).wait_recv()
+    launch(to_core(11, wd.at[over * 2 + swap]))
+    cross(4)
+    for index, slot in enumerate((
+        here * 2 + same, down * 2 + same, up * 2 + same, here * 2 + swap,
+        over * 2 + same, up * 2 + swap, down * 2 + swap, over * 2 + swap,
+    )):
+        to_core(4 + index, wd.at[slot + 2 * mirror]).wait_recv()
+
+    middle(0)
+    middle(1)
+    cross(5)
+    middle(2)
+    middle(3)
+    late(0, 2)
+    cross(6)
+    late(2, 2)
+    last(0, 2)
+    late(4, 2)
+    cross(7)
+    last(2, 2)
+    last(4, 2)
+    late(6)
+    last(6)
+    late(7)
+    last(7)
 
     full = facc[...]
     x1 = full.astype(jnp.bfloat16)
@@ -308,8 +363,8 @@
         peer = lax.rem(ga + k, 16)
         remote(red_src.at[peer], red_a.at[k - 1], r1s, r1r, (peer, ba)).start()
 
-    for h in range(2):
-        wait_bytes(wf.at[here, part[h]], w1s.at[h])
+    wait_bytes(wn.at[here], w1s.at[0])
+    wait_bytes(wd.at[own], w1s.at[1])
     for cp in sends:
         cp.wait_send()
 
@@ -357,7 +412,9 @@
         scratch_shapes=[
             pltpu.VMEM((7, 1024, GB), jnp.bfloat16),
             pltpu.VMEM((7, GB, GB), jnp.bfloat16),
-            pltpu.VMEM((8, NBLK, 64, GB), jnp.bfloat16),
+            pltpu.VMEM((8, NEAR, 64, GB), jnp.bfloat16),
+            pltpu.VMEM((16, FAR, 32, GB), jnp.bfloat16),
+            pltpu.VMEM((FAR, 32, GB), jnp.bfloat16),
             pltpu.VMEM((GB, 1024), jnp.float32),
             pltpu.VMEM((GB, 1024), jnp.float32),
             pltpu.VMEM((GB, 1024), jnp.float32),
@@ -370,7 +427,7 @@
             pltpu.VMEM((15, 2, 128), jnp.float32),
             pltpu.VMEM((16, 2, 128), jnp.float32),
             dma((6, 2 * NCH)), dma((6, 2 * NCH)), dma, dma((7,)), dma,
-            pltpu.SemaphoreType.REGULAR((4,)), dma((2,)), dma((2,)), dma((6,)), dma((6,)), dma((8,)), dma((8,)),
+            pltpu.SemaphoreType.REGULAR((4,)), dma((2,)), dma((2,)), dma((4,)), dma((4,)), dma((9,)), dma((9,)), dma((12,)), dma((12,)),
             dma, dma, dma, dma,
         ],
         compiler_params=pltpu.CompilerParams(

time: 82.5 us -> 79.2 us (0.960)
  Pallas kernels: 81.1 us -> 77.8 us
    pallas_call x1, Pallas kernels: 81.1 us -> 77.8 us  [shards(): pl.pallas_call(kernel, out_shape=jax.ShapeDtypeStruct((2, 126), jnp.float...]
where the time goes in v6:
time: 79.2 us; the launch traced here: 79.1 us
  Pallas kernels  77.8 us (98%)
  local copies, waits for them, and re-layouts  1.24 us (2%)
    pallas_call x1, Pallas kernels, shards(): pl.pallas_call(kernel, out_shape=jax.ShapeDtypeStruct((2, 126), jnp.float...  77.8 us

profile of v6, /device:TPU:1, one launch (start us, length us, event | category | flops | bytes accessed | tf_op | source)
XLA Modules:
  0.0 79.1 jit_solution(1574240446525804908)
XLA Ops:
  0.0 77.8 %self_energy.1 = f32[2,126]{1,0:T(2,128)} custom-call(bf16[1024,512]{1,0:T(8,128)(2,1)} %bitcast.1, bf16[8192,512]{1,0:T(8,128)(2,1)} %w_ref.1, f32[2,16]{1,0:T(2,128)} %bf_ref.1, s32[2,2016]{1,0:T(2,128)} %pair_ref.1), custom_call_target="tpu_custom_call" | custom-call | flops 8999999488 | bytes 20971520 | tf_op jit(solution)/shard_map/self_energy/pallas_call | solution.py:402
  77.8 1.2 %copy.6 = f32[2,126]{1,0:T(2,128)} copy(f32[2,126]{1,0:T(2,128)} %self_energy.1) | data formatting | bytes 2016

commit v7 on v6

--- a/solution.py
+++ b/solution.py
@@ -130,16 +130,15 @@
     give_far((gai(-1), ba), own, gai(-3), 0)
     give_far((gai(1), ba), own, gai(3), 1)
     give_far((gai(1), ba), own, gai(3, 1), 2)
-    first(1)
-    first(2)
     pl.semaphore_wait(known.at[0], 7)
     greet(known.at[1])
     give_far((gai(2), ba), own, gai(4), 3)
     give_far((gai(2), ba), own, gai(4, 1), 4)
+    first(1)
     pl.semaphore_wait(known.at[1], 7)
     greet(known.at[2])
     give_far((gai(-2, 1), bai(0, 1, c)), here * 2 + swap, gai(-3, 1), 5)
-    for k in range(3, NCH):
+    for k in range(2, NCH):
         first(k)
 
     own_p.wait()
@@ -334,16 +333,16 @@
     middle(1)
     cross(5)
     middle(2)
-    middle(3)
     late(0, 2)
+    last(0, 2)
     cross(6)
     late(2, 2)
-    last(0, 2)
+    middle(3)
     late(4, 2)
     cross(7)
     last(2, 2)
+    late(6)
     last(4, 2)
-    late(6)
     last(6)
     late(7)
     last(7)
@@ -380,35 +379,33 @@
     mine = red_src[ga]
     for k in range(15):
         mine += red_a[k]
-    red_b[ba] = mine
+    red_b[...] = mine
+    keep = pltpu.make_async_copy(red_b, out_ref.at[ba], ploc)
+    keep.start()
 
     for k in FAR_FIRST:
         peer = lax.rem(ba + k, 16)
-        remote(red_b.at[ba], red_b.at[ba], r2s, r2r, (ga, peer)).start()
+        remote(red_b, out_ref.at[ba], r2s, r2r, (ga, peer)).start()
 
     wait_bytes(red_a, r1s)
-    wait_bytes(red_b.at[pl.ds(0, 15)], r2r)
-    total = red_b[0]
-    for k in range(1, 16):
-        total += red_b[k]
-    out_ref[...] = total[:, :126]
-
-    wait_bytes(red_b.at[pl.ds(0, 15)], r2s)
+    keep.wait()
+    wait_bytes(red_a, r2s)
+    wait_bytes(out_ref.at[pl.ds(0, 15)], r2r)
 
 
 def shards(matrix_elements, screening, band_factor, pair_list):
     bands, quasi, width = matrix_elements.shape
     dma = pltpu.SemaphoreType.DMA
-    return pl.pallas_call(
+    parts = pl.pallas_call(
         kernel,
-        out_shape=jax.ShapeDtypeStruct((2, 126), jnp.float32),
+        out_shape=jax.ShapeDtypeStruct((16, 2, 128), jnp.float32),
         in_specs=[
             pl.BlockSpec(memory_space=pltpu.HBM),
             pl.BlockSpec(memory_space=pltpu.HBM),
             pl.BlockSpec(memory_space=pltpu.SMEM),
             pl.BlockSpec(memory_space=pltpu.HBM),
         ],
-        out_specs=pl.BlockSpec(memory_space=pltpu.VMEM),
+        out_specs=pl.BlockSpec(memory_space=pltpu.HBM),
         scratch_shapes=[
             pltpu.VMEM((7, 1024, GB), jnp.bfloat16),
             pltpu.VMEM((7, GB, GB), jnp.bfloat16),
@@ -425,7 +422,7 @@
             pltpu.VMEM((128, 128), jnp.float32),
             pltpu.VMEM((16, 2, 128), jnp.float32),
             pltpu.VMEM((15, 2, 128), jnp.float32),
-            pltpu.VMEM((16, 2, 128), jnp.float32),
+            pltpu.VMEM((2, 128), jnp.float32),
             dma((6, 2 * NCH)), dma((6, 2 * NCH)), dma, dma((7,)), dma,
             pltpu.SemaphoreType.REGULAR((4,)), dma((2,)), dma((2,)), dma((4,)), dma((4,)), dma((9,)), dma((9,)), dma((12,)), dma((12,)),
             dma, dma, dma, dma,
@@ -436,6 +433,7 @@
         cost_estimate=pl.CostEstimate(flops=9 * 10**9, bytes_accessed=20 << 20, transcendentals=0),
         name="self_energy",
     )(matrix_elements.reshape(bands * quasi, width), screening, band_factor, pair_list)
+    return jnp.sum(parts, axis=0)[:, :126]
 
 
 def solution(mesh):

time: 79.2 us -> 78.8 us (level)
  other arithmetic: 0 us -> 1.31 us
  local copies, waits for them, and re-layouts: 1.24 us -> 0 us
    reduce_sum x0 -> x1, other arithmetic: none -> 1.31 us  [shards(): return jnp.sum(parts, axis=0)[:, :126]]
    unnamed x1 -> x0, local copies, waits for them, and re-layouts: 1.24 us -> none
where the time goes in v7:
time: 78.8 us; the launch traced here: 78.6 us
  Pallas kernels  77.3 us (98%)
  other arithmetic  1.31 us (2%)
    pallas_call x1, Pallas kernels, shards(): pl.pallas_call(kernel, out_shape=jax.ShapeDtypeStruct((16, 2, 128), jnp.f...  77.3 us

profile of v7, /device:TPU:1, one launch (start us, length us, event | category | flops | bytes accessed | tf_op | source)
XLA Modules:
  0.0 78.6 jit_solution(14461679209871167131)
XLA Ops:
  0.0 77.3 %self_energy.1 = f32[16,2,128]{2,1,0:T(2,128)} custom-call(bf16[1024,512]{1,0:T(8,128)(2,1)} %bitcast.2, bf16[8192,512]{1,0:T(8,128)(2,1)} %w_ref.1, f32[2,16]{1,0:T(2,128)} %bf_ref.1, s32[2,2016]{1,0:T(2,128)} %pair_ref.1), custom_call_target="tpu_custom_call" | custom-call | flops 8999999488 | bytes 20971520 | tf_op jit(solution)/shard_map/self_energy/pallas_call | solution.py:399
  77.3 1.3 %reduce_sum.9 = f32[2,128]{1,0:T(2,128)} reduce(f32[16,2,128]{2,1,0:T(2,128)} %self_energy.1, f32[]{:T(128)} %constant.0.clone.1), dimensions={0}, to_apply=%region_0.0 | reduce | flops 3840 | bytes 17412 | tf_op jit(solution)/shard_map/reduce_sum | solution.py:436

commit v8 on v7

--- a/solution.py
+++ b/solution.py
@@ -43,9 +43,9 @@
 
 
 def kernel(
-    m_ref, w_ref, bf_ref, pair_ref, out_ref,
-    mv, wown, wn, wd, stage, t2, tm2, tb2, ab2, pairs, pp, one_n, facc, red_src, red_a, red_b,
-    msend, mrecv, mloc, wloc, ploc, known, w1s, w1r, xs, xr, w2s, w2r, w3s, w3r, r1s, r1r, r2s, r2r,
+    m_ref, w_ref, factor_ref, pair_ref, out_ref,
+    mv, wown, wn, wd, stage, t2, tm2, tb2, ab2, bf_ref, pairs, pp, one_n, facc, red_src, red_a, red_b,
+    msend, mrecv, mloc, wloc, ploc, floc, known, w1s, w1r, xs, xr, w2s, w2r, w3s, w3r, r1s, r1r, r2s, r2r,
 ):
     ga, ba = lax.axis_index("ga"), lax.axis_index("ba")
     z, s = ga // 2, lax.rem(ga, 2)
@@ -70,20 +70,6 @@
             pl.semaphore_signal(sem, inc=1, device_id=device, device_id_type=MESH)
 
     greet(barrier)
-
-    own_p = pltpu.make_async_copy(pair_ref, pairs, ploc)
-    own_p.start()
-    own_m = pltpu.make_async_copy(m_ref, mv.at[A0], mloc)
-    own_m.start()
-    own_rows = (
-        (A0, gai(0)), (A1, gai(1)), (AM1, gai(-1)), (A2, gai(2)), (AM2, gai(-2)),
-        (B0, gai(0, 1)), (B2, gai(2, 1)),
-    )
-    own_w = []
-    for slot, block in own_rows:
-        cp = pltpu.make_async_copy(w_ref.at[pl.ds(block * GB, GB)], wown.at[slot], wloc.at[slot])
-        cp.start()
-        own_w.append(cp)
 
     def hop(flow, k):
         size = CH // 2 if flow in (DN2, X2) else CH
@@ -121,8 +107,8 @@
         ).start()
 
     pl.semaphore_wait(barrier, 7)
+    first(0)
     greet(known.at[0])
-    first(0)
     own = here * 2 + same
     give_near(gai(-1, 1), 0)
     give_near(gai(1, 1), 1)
@@ -140,6 +126,22 @@
     give_far((gai(-2, 1), bai(0, 1, c)), here * 2 + swap, gai(-3, 1), 5)
     for k in range(2, NCH):
         first(k)
+
+    own_p = pltpu.make_async_copy(pair_ref, pairs, ploc)
+    own_p.start()
+    own_m = pltpu.make_async_copy(m_ref, mv.at[A0], mloc)
+    own_m.start()
+    own_rows = (
+        (A0, gai(0)), (A1, gai(1)), (AM1, gai(-1)), (A2, gai(2)), (AM2, gai(-2)),
+        (B0, gai(0, 1)), (B2, gai(2, 1)),
+    )
+    own_w = []
+    for slot, block in own_rows:
+        cp = pltpu.make_async_copy(w_ref.at[pl.ds(block * GB, GB)], wown.at[slot], wloc.at[slot])
+        cp.start()
+        own_w.append(cp)
+    own_f = pltpu.make_async_copy(factor_ref, bf_ref, floc)
+    own_f.start()
 
     own_p.wait()
     pp[...] = jnp.full(pp.shape, -1, jnp.int32)
@@ -279,6 +281,7 @@
     fwd(4)
     hop(X0, 6).start()
     hop(X0, 7).start()
+    own_f.wait()
     own_m.wait()
     for cp in own_w:
         cp.wait()
@@ -402,7 +405,7 @@
         in_specs=[
             pl.BlockSpec(memory_space=pltpu.HBM),
             pl.BlockSpec(memory_space=pltpu.HBM),
-            pl.BlockSpec(memory_space=pltpu.SMEM),
+            pl.BlockSpec(memory_space=pltpu.HBM),
             pl.BlockSpec(memory_space=pltpu.HBM),
         ],
         out_specs=pl.BlockSpec(memory_space=pltpu.HBM),
@@ -416,6 +419,7 @@
             pltpu.VMEM((GB, 1024), jnp.float32),
             pltpu.VMEM((GB, 1024), jnp.float32),
             pltpu.VMEM((1024, GB), jnp.float32),
+            pltpu.SMEM((2, 16), jnp.float32),
             pltpu.VMEM((2, 2016), jnp.int32),
             pltpu.VMEM((2, 2048), jnp.int32),
             pltpu.VMEM((128, 2048), jnp.bfloat16),
@@ -423,7 +427,7 @@
             pltpu.VMEM((16, 2, 128), jnp.float32),
             pltpu.VMEM((15, 2, 128), jnp.float32),
             pltpu.VMEM((2, 128), jnp.float32),
-            dma((6, 2 * NCH)), dma((6, 2 * NCH)), dma, dma((7,)), dma,
+            dma((6, 2 * NCH)), dma((6, 2 * NCH)), dma, dma((7,)), dma, dma,
             pltpu.SemaphoreType.REGULAR((4,)), dma((2,)), dma((2,)), dma((4,)), dma((4,)), dma((9,)), dma((9,)), dma((12,)), dma((12,)),
             dma, dma, dma, dma,
         ],

time: 78.8 us -> 78.1 us (level)
  no operation moved by 1% of the time
where the time goes in v8:
time: 78.1 us; the launch traced here: 77.9 us
  Pallas kernels  76.6 us (98%)
  other arithmetic  1.31 us (2%)
    pallas_call x1, Pallas kernels, shards(): pl.pallas_call(kernel, out_shape=jax.ShapeDtypeStruct((16, 2, 128), jnp.f...  76.6 us

profile of v8, /device:TPU:1, one launch (start us, length us, event | category | flops | bytes accessed | tf_op | source)
XLA Modules:
  0.0 77.9 jit_solution(9002856505696890267)
XLA Ops:
  0.0 76.6 %self_energy.1 = f32[16,2,128]{2,1,0:T(2,128)} custom-call(bf16[1024,512]{1,0:T(8,128)(2,1)} %bitcast.2, bf16[8192,512]{1,0:T(8,128)(2,1)} %w_ref.1, f32[2,16]{1,0:T(2,128)} %factor_ref.1, s32[2,2016]{1,0:T(2,128)} %pair_ref.1), custom_call_target="tpu_custom_call" | custom-call | flops 8999999488 | bytes 20971520 | tf_op jit(solution)/shard_map/self_energy/pallas_call | solution.py:402
  76.6 1.3 %reduce_sum.9 = f32[2,128]{1,0:T(2,128)} reduce(f32[16,2,128]{2,1,0:T(2,128)} %self_energy.1, f32[]{:T(128)} %constant.0.clone.1), dimensions={0}, to_apply=%region_0.0 | reduce | flops 3840 | bytes 17412 | tf_op jit(solution)/shard_map/reduce_sum | solution.py:440

commit v9 on v8

--- a/solution.py
+++ b/solution.py
@@ -70,16 +70,19 @@
             pl.semaphore_signal(sem, inc=1, device_id=device, device_id_type=MESH)
 
     greet(barrier)
+    own_m = pltpu.make_async_copy(m_ref, mv.at[A0], mloc)
+    own_m.start()
 
     def hop(flow, k):
         size = CH // 2 if flow in (DN2, X2) else CH
         rows = pl.ds(pl.multiple_of(k * size, size), size)
+        own_block = m_ref if isinstance(k, int) and k == 0 else mv.at[A0]
         src, dst, target = {
-            UP1: (m_ref, AM1, gai(1)),
-            DN1: (m_ref, A1, gai(-1)),
+            UP1: (own_block, AM1, gai(1)),
+            DN1: (own_block, A1, gai(-1)),
             UP2: (mv.at[AM1], AM2, gai(1)),
             DN2: (mv.at[A1], A2, gai(-1)),
-            X0: (m_ref, B0, gai(0, 1)),
+            X0: (own_block, B0, gai(0, 1)),
             X2: (mv.at[A2], B2, gai(0, 1)),
         }[flow]
         return remote(
@@ -120,6 +123,7 @@
     greet(known.at[1])
     give_far((gai(2), ba), own, gai(4), 3)
     give_far((gai(2), ba), own, gai(4, 1), 4)
+    own_m.wait()
     first(1)
     pl.semaphore_wait(known.at[1], 7)
     greet(known.at[2])
@@ -129,8 +133,6 @@
 
     own_p = pltpu.make_async_copy(pair_ref, pairs, ploc)
     own_p.start()
-    own_m = pltpu.make_async_copy(m_ref, mv.at[A0], mloc)
-    own_m.start()
     own_rows = (
         (A0, gai(0)), (A1, gai(1)), (AM1, gai(-1)), (A2, gai(2)), (AM2, gai(-2)),
         (B0, gai(0, 1)), (B2, gai(2, 1)),
@@ -282,7 +284,6 @@
     hop(X0, 6).start()
     hop(X0, 7).start()
     own_f.wait()
-    own_m.wait()
     for cp in own_w:
         cp.wait()
     early(0)

time: 78.1 us -> 78.1 us (level)
  no operation moved by 1% of the time
where the time goes in v9:
time: 78.1 us; the launch traced here: 77.9 us
  Pallas kernels  76.6 us (98%)
  other arithmetic  1.31 us (2%)
    pallas_call x1, Pallas kernels, shards(): pl.pallas_call(kernel, out_shape=jax.ShapeDtypeStruct((16, 2, 128), jnp.f...  76.6 us

profile of v9, /device:TPU:1, one launch (start us, length us, event | category | flops | bytes accessed | tf_op | source)
XLA Modules:
  0.0 77.9 jit_solution(13758777105717798813)
XLA Ops:
  0.0 76.6 %self_energy.1 = f32[16,2,128]{2,1,0:T(2,128)} custom-call(bf16[1024,512]{1,0:T(8,128)(2,1)} %bitcast.2, bf16[8192,512]{1,0:T(8,128)(2,1)} %w_ref.1, f32[2,16]{1,0:T(2,128)} %factor_ref.1, s32[2,2016]{1,0:T(2,128)} %pair_ref.1), custom_call_target="tpu_custom_call" | custom-call | flops 8999999488 | bytes 20971520 | tf_op jit(solution)/shard_map/self_energy/pallas_call | solution.py:403
  76.6 1.3 %reduce_sum.9 = f32[2,128]{1,0:T(2,128)} reduce(f32[16,2,128]{2,1,0:T(2,128)} %self_energy.1, f32[]{:T(128)} %constant.0.clone.1), dimensions={0}, to_apply=%region_0.0 | reduce | flops 3840 | bytes 17412 | tf_op jit(solution)/shard_map/reduce_sum | solution.py:441
